TPU v7x, 128 devices: a whole 4x4x4 slice. The times are simulated.
128 devices in a mesh: seq: 8 (over y, z_hi), head: 16 (over x, z_lo, core).
Axes of the slice: x: 4, y: 4, z: 4 (z_hi: 2, z_lo: 2; z = z_hi * 2 + z_lo), core: 2. Of those that a mesh axis runs over, the one named last changes fastest.
Arguments:
- sequence_activity: bfloat16 [2, 4096, 4096], P(None, 'seq', 'head'), may hold values from -6 to 6
- lookup_mapping_tensor: bfloat16 [4096, 16, 768], P(None, 'head'), may hold values from -1 to 1, as said below
- stepsize_mapping_matrix: bfloat16 [4096, 16], P(None, 'head'), may hold values from -0.09375 to 0.09375
- logit_sharpness: float32 [16], P('head'), may hold values from 4 to 120
- adapter_gain_vector: float32 [16, 256], P('head'), may hold values from 0.1 to 1.9
- starting_inner_left_matrix: float32 [16, 256, 512], P('head'), may hold values from -0.375 to 0.375
- starting_inner_right_matrix: float32 [16, 512, 256], P('head'), may hold values from -0.25 to 0.25
- final_mixing_matrix: bfloat16 [16, 256, 4096], P('head'), may hold values from -0.09375 to 0.09375
Outputs:
- mixed: bfloat16 [2, 4096, 4096], P(None, 'seq', 'head')
Inputs may be any that keep to these rules, and one draw needn't show every extreme that they name: `lookup_mapping_tensor`: entries of order 1 / sqrt(4096).
All inputs are finite; a program needn't handle non-finite values.
Results may differ from a plain program's by a relative error of at most 0.02.
Values may be sent and summed in bfloat16 or wider, within the bound.
A program may use at most 64 MiB of HBM per device.

v0:
```python
import jax
import jax.numpy as jnp
from jax import lax
from jax.sharding import PartitionSpec as P

WIN = 2048
NS_STEPS = 3


update_rate = 0.3


def shifted(block, axis, distance):
    devices = range(lax.axis_size(axis))
    route = [(i - distance, i) for i in devices if i - distance in devices]
    return lax.ppermute(block, axis, route)


def orthogonalize(update):
    scale = lax.rsqrt(jnp.sum(update * update) + 1e-06)
    current = update * scale
    for sweep in range(NS_STEPS):
        if current.shape[0] <= current.shape[1]:
            gram = jnp.dot(current, current.T, precision=lax.Precision.HIGHEST)
            current = 1.5 * current - 0.5 * jnp.dot(gram, current, precision=lax.Precision.HIGHEST)
        else:
            gram = jnp.dot(current.T, current, precision=lax.Precision.HIGHEST)
            current = 1.5 * current - 0.5 * jnp.dot(current, gram, precision=lax.Precision.HIGHEST)
    return current


def fast_group(weight_in, weight_out, keys, weighted, query_rows):
    in_half = weight_in.astype(jnp.bfloat16)
    out_half = weight_out.astype(jnp.bfloat16)
    hidden = jnp.dot(keys, in_half, preferred_element_type=jnp.float32)
    gating = jax.nn.sigmoid(hidden)
    activated = (hidden * gating).astype(jnp.bfloat16)
    grad_out = jnp.dot(activated.T, weighted, preferred_element_type=jnp.float32)
    backward = jnp.dot(weighted, out_half.T, preferred_element_type=jnp.float32)
    slopes = (backward * gating * (1.0 + hidden * (1.0 - gating))).astype(jnp.bfloat16)
    grad_in = jnp.dot(keys.T, slopes, preferred_element_type=jnp.float32)
    new_in = weight_in + update_rate * orthogonalize(grad_in)
    new_out = weight_out + update_rate * orthogonalize(grad_out)
    query_hidden = jnp.dot(
        query_rows, new_in.astype(jnp.bfloat16), preferred_element_type=jnp.float32
    )
    query_act = jax.nn.silu(query_hidden).astype(jnp.bfloat16)
    fast = jnp.dot(query_act, new_out.astype(jnp.bfloat16), preferred_element_type=jnp.float32)
    return (new_in, new_out, fast)


def prepare(projected, rate_col, count_seqs):
    head_dim = projected.shape[1] // 3
    query_rows = projected[:, :head_dim]
    keys = projected[:, head_dim : 2 * head_dim]
    values = projected[:, 2 * head_dim :]
    query_norm = (
        query_rows * lax.rsqrt(jnp.sum(query_rows * query_rows, axis=1, keepdims=True) + 1e-06)
    ).astype(jnp.bfloat16)
    key_norm = (keys * lax.rsqrt(jnp.sum(keys * keys, axis=1, keepdims=True) + 1e-06)).astype(
        jnp.bfloat16
    )
    value_half = values.astype(jnp.bfloat16)
    weighted = (jax.nn.softplus(rate_col) * values).astype(jnp.bfloat16)
    return (
        query_norm.reshape(count_seqs, -1, head_dim),
        key_norm.reshape(count_seqs, -1, head_dim),
        value_half.reshape(count_seqs, -1, head_dim),
        weighted.reshape(count_seqs, -1, head_dim),
    )


def attend_window(query_rows, keys, values, scale, start):
    count = query_rows.shape[1]
    window = keys.shape[1] - count
    scores = scale * jnp.einsum(
        "sqd,skd->sqk", query_rows, keys, preferred_element_type=jnp.float32
    )
    row_pos = lax.broadcasted_iota(jnp.int32, (count, count + window), 0)
    col_pos = lax.broadcasted_iota(jnp.int32, (count, count + window), 1)
    valid = (col_pos >= row_pos) & (col_pos <= row_pos + window) & (col_pos + start >= window)
    scores = jnp.where(valid[None], scores, -1e30)
    highest = jnp.max(scores, axis=2, keepdims=True)
    weights = jnp.exp(scores - highest)
    probs = (weights / jnp.sum(weights, axis=2, keepdims=True)).astype(jnp.bfloat16)
    return jnp.einsum("sqk,skd->sqd", probs, values, preferred_element_type=jnp.float32)


def combine(attended_output, fast, gain):
    normed = fast * lax.rsqrt(jnp.mean(fast * fast, axis=-1, keepdims=True) + 1e-05) * gain
    return (attended_output + normed).astype(jnp.bfloat16)


def body(
    sequence_activity,
    lookup_mapping_tensor,
    stepsize_mapping_matrix,
    logit_sharpness,
    adapter_gain_vector,
    starting_inner_left_matrix,
    starting_inner_right_matrix,
    final_mixing_matrix,
):
    seqs, head_group, local_width = sequence_activity.shape
    total_rows = seqs * head_group
    flattened = sequence_activity.reshape(total_rows, local_width)
    weights_in = lookup_mapping_tensor.reshape(
        lookup_mapping_tensor.shape[0], lookup_mapping_tensor.shape[2]
    )
    head_dim = weights_in.shape[1] // 3
    piece = lax.all_gather(flattened, "head", axis=1, tiled=True)
    projected = jnp.dot(piece, weights_in, preferred_element_type=jnp.float32)
    rate_col = jnp.dot(piece, stepsize_mapping_matrix, preferred_element_type=jnp.float32)
    query_rows, keys, values, weighted = prepare(projected, rate_col, seqs)
    token_position = lax.axis_index("seq")
    length = lax.axis_size("seq")
    reach = WIN // head_group
    hops = min(reach, length - 1)
    earlier = []
    current = (keys, values)
    for distance in range(hops):
        current = shifted((current[0], current[1]), "seq", 1)
        earlier.insert(0, current)
    windowed_key_rows = jnp.concatenate([pair[0] for pair in earlier] + [keys], axis=1)
    windowed_value_rows = jnp.concatenate([pair[1] for pair in earlier] + [values], axis=1)
    attended_output = attend_window(
        query_rows,
        windowed_key_rows,
        windowed_value_rows,
        logit_sharpness[0],
        token_position * head_group,
    )
    start_in = starting_inner_left_matrix[0]
    start_out = starting_inner_right_matrix[0]

    def turn(step, carry):
        held_in, held_out, fast_all = carry
        which = step // length
        live = step % length == token_position
        which = jnp.clip(which, 0, seqs - 1)
        use_in = jnp.where(token_position == 0, start_in, held_in)
        use_out = jnp.where(token_position == 0, start_out, held_out)
        block_keys = lax.dynamic_index_in_dim(keys, which, 0, keepdims=False)
        block_weighted = lax.dynamic_index_in_dim(weighted, which, 0, keepdims=False)
        block_queries = lax.dynamic_index_in_dim(query_rows, which, 0, keepdims=False)

        def working():
            return fast_group(use_in, use_out, block_keys, block_weighted, block_queries)

        def resting():
            return (use_in, use_out, jnp.zeros((head_group, head_dim), jnp.float32))

        new_in, new_out, fast = lax.cond(live, working, resting)
        stored = lax.dynamic_update_index_in_dim(fast_all, fast, which, 0)
        fast_all = jnp.where(live, stored, fast_all)
        sent_in, sent_out = shifted((new_in, new_out), "seq", 1)
        return (sent_in, sent_out, fast_all)

    turns = seqs * length
    carried = (start_in, start_out, jnp.zeros((seqs, head_group, head_dim), jnp.float32))
    carried = lax.fori_loop(0, turns, turn, carried)
    head_out = combine(attended_output, carried[2], adapter_gain_vector[0]).reshape(
        total_rows, head_dim
    )
    partial_value = jnp.dot(head_out, final_mixing_matrix[0], preferred_element_type=jnp.float32)
    result = lax.psum_scatter(
        partial_value.astype(jnp.bfloat16), "head", scatter_dimension=1, tiled=True
    )
    return result.reshape(seqs, head_group, -1)


def solution(mesh):
    in_specs = (
        P(None, "seq", "head"),
        P(None, "head", None),
        P(None, "head"),
        P("head"),
        P("head", None),
        P("head", None, None),
        P("head", None, None),
        P("head", None, None),
    )
    out_specs = P(None, "seq", "head")
    return jax.shard_map(body, mesh=mesh, in_specs=in_specs, out_specs=out_specs, check_vma=False)
```

profile of v0, /device:TPU:16, one launch (start us, length us, event | category | flops | bytes accessed | tf_op | source)
XLA Modules:
  0.0 1016.0 jit_solution(2209123766878446001)
XLA Ops:
  7.3 64.5 %all-gather.2.cloned.1.call-done = bf16[1024,4096]{1,0:T(8,128)(2,1)} async-done(((bf16[1024,256]{1,0:T(8,128)(2,1)}), bf16[1024,4096]{1,0:T(8,128)(2,1)}) %all-gather.2.cloned.1.call-update) | async-done | bytes 8388624 | tf_op jit(solution)/shard_map/all_gather | solution.py:111
  71.8 5.8 fusion.87
  77.6 9.0 fusion.61
  96.6 9.1 collective-permute-done.6
  120.5 7.8 collective-permute-done.7
  143.1 7.7 collective-permute-done.8
  155.5 692.3 %while.19 = (s32[]{:T(128)}, f32[256,512]{1,0:T(8,128)}, f32[512,256]{1,0:T(8,128)}, f32[2,512,256]{2,1,0:T(8,128)}, s32[]{:T(128)}, /*index=5*/pred[]{:T(512)},...) while((s32[]{:T(128)}, f32[256,512]{1,0:T(8,128)}, ...), condition=%wide.region_9.10_spmd, body=%wide.region_4.9_spmd.sunk | while | flops 5647237120 | bytes 32771644 | solution.py:161
  168.6 15.8 %collective-permute-done = f32[256,512]{1,0:T(8,128)} collective-permute-done((f32[256,512]{1,0:T(8,128)S(1)}, f32[256,512]{1,0:T(8,128)}, u32[]{:S(2)}, u32[]{:S(2)}) %collective-permute-start) | collective-permute-done | bytes 524320 | tf_op jit(solution)/shard_map/while/body/eval_jaxpr/ppermute | solution.py:16
  184.5 10.6 %collective-permute-done.1 = f32[512,256]{1,0:T(8,128)} collective-permute-done((f32[512,256]{1,0:T(8,128)S(1)}, f32[512,256]{1,0:T(8,128)}, u32[]{:S(2)}, u32[]{:S(2)}) %collective-permute-start.1) | collective-permute-done | bytes 524320 | tf_op jit(solution)/shard_map/while/body/eval_jaxpr/ppermute | solution.py:16
  208.1 9.3 collective-permute-done
  217.5 9.6 collective-permute-done.1
  240.2 9.3 collective-permute-done
  249.5 8.7 collective-permute-done.1
  263.3 6.1 collective-permute-start.1
  271.3 82.9 %collective-permute-done = f32[256,512]{1,0:T(8,128)} collective-permute-done((f32[256,512]{1,0:T(8,128)S(1)}, f32[256,512]{1,0:T(8,128)}, u32[]{:S(2)}, u32[]{:S(2)}) %collective-permute-start) | collective-permute-done | bytes 524320 | tf_op jit(solution)/shard_map/while/body/eval_jaxpr/ppermute | solution.py:16
  354.2 7.0 collective-permute-done.1
  363.5 24.5 %conditional.2 = (f32[256,512]{1,0:T(8,128)S(1)}, f32[512,256]{1,0:T(8,128)S(1)}, f32[1,512,256]{2,1,0:T(8,128)}) conditional(s32[]{:T(128)} %convert_element_type.110, (f32[256,512]{1,0:T(8,128)S(1)}, f32[512,256]{1,0:T(8,128)S(1)}) %tuple.60, (bf16[2,512,256]{2,1,0:T(8,128)(2,1)}, s32[]{:T(128)}, bf16[2,512,256]{2,1,0:T(8,128)(2,1)}, ...), branch_computations={%region_5.5_spmd, %region_6.8_spmd} | conditional | flops 5646843904 | bytes 23857780 | solution.py:153
  394.0 13.3 %collective-permute-done = f32[256,512]{1,0:T(8,128)} collective-permute-done((f32[256,512]{1,0:T(8,128)S(1)}, f32[256,512]{1,0:T(8,128)}, u32[]{:S(2)}, u32[]{:S(2)}) %collective-permute-start) | collective-permute-done | bytes 524320 | tf_op jit(solution)/shard_map/while/body/eval_jaxpr/ppermute | solution.py:16
  407.3 6.1 collective-permute-done.1
  416.6 24.9 %collective-permute-start = (f32[256,512]{1,0:T(8,128)S(1)}, f32[256,512]{1,0:T(8,128)}, u32[]{:S(2)}, u32[]{:S(2)}) collective-permute-start(f32[256,512]{1,0:T(8,128)S(1)} %get-tuple-element.431), channel_id=1, source_target_pairs={{0,16},{16,32},{32,48},{48,64},{64,80},{80,96},{96,112},{1,17},{17... | collective-permute-start | bytes 1572872 | tf_op jit(solution)/shard_map/while/body/eval_jaxpr/ppermute | solution.py:16
  445.4 8.4 collective-permute-done
  462.5 6.0 collective-permute-start
  468.5 26.7 %collective-permute-start.1 = (f32[512,256]{1,0:T(8,128)S(1)}, f32[512,256]{1,0:T(8,128)}, u32[]{:S(2)}, u32[]{:S(2)}) collective-permute-start(f32[512,256]{1,0:T(8,128)S(1)} %get-tuple-element.432), channel_id=1, source_target_pairs={{0,16},{16,32},{32,48},{48,64},{64,80},{80,96},{96,112},{1,17},{17... | collective-permute-start | bytes 1572872 | tf_op jit(solution)/shard_map/while/body/eval_jaxpr/ppermute | solution.py:16
  505.1 10.5 %collective-permute-start = (f32[256,512]{1,0:T(8,128)S(1)}, f32[256,512]{1,0:T(8,128)}, u32[]{:S(2)}, u32[]{:S(2)}) collective-permute-start(f32[256,512]{1,0:T(8,128)S(1)} %get-tuple-element.431), channel_id=1, source_target_pairs={{0,16},{16,32},{32,48},{48,64},{64,80},{80,96},{96,112},{1,17},{17... | collective-permute-start | bytes 1572872 | tf_op jit(solution)/shard_map/while/body/eval_jaxpr/ppermute | solution.py:16
  515.6 6.9 collective-permute-start.1
  536.1 21.2 %collective-permute-start = (f32[256,512]{1,0:T(8,128)S(1)}, f32[256,512]{1,0:T(8,128)}, u32[]{:S(2)}, u32[]{:S(2)}) collective-permute-start(f32[256,512]{1,0:T(8,128)S(1)} %get-tuple-element.431), channel_id=1, source_target_pairs={{0,16},{16,32},{32,48},{48,64},{64,80},{80,96},{96,112},{1,17},{17... | collective-permute-start | bytes 1572872 | tf_op jit(solution)/shard_map/while/body/eval_jaxpr/ppermute | solution.py:16
  557.3 9.9 collective-permute-start.1
  569.1 6.1 collective-permute-done.1
  578.4 7.7 collective-permute-start
  586.1 6.9 collective-permute-start.1
  597.7 6.0 collective-permute-done.1
  611.9 5.9 collective-permute-start.1
  619.8 5.8 collective-permute-done
  625.6 5.6 collective-permute-done.1
  643.7 39.7 %collective-permute-done = f32[256,512]{1,0:T(8,128)} collective-permute-done((f32[256,512]{1,0:T(8,128)S(1)}, f32[256,512]{1,0:T(8,128)}, u32[]{:S(2)}, u32[]{:S(2)}) %collective-permute-start) | collective-permute-done | bytes 524320 | tf_op jit(solution)/shard_map/while/body/eval_jaxpr/ppermute | solution.py:16
  683.4 5.6 collective-permute-done.1
  691.3 24.5 %conditional.2 = (f32[256,512]{1,0:T(8,128)S(1)}, f32[512,256]{1,0:T(8,128)S(1)}, f32[1,512,256]{2,1,0:T(8,128)}) conditional(s32[]{:T(128)} %convert_element_type.110, (f32[256,512]{1,0:T(8,128)S(1)}, f32[512,256]{1,0:T(8,128)S(1)}) %tuple.60, (bf16[2,512,256]{2,1,0:T(8,128)(2,1)}, s32[]{:T(128)}, bf16[2,512,256]{2,1,0:T(8,128)(2,1)}, ...), branch_computations={%region_5.5_spmd, %region_6.8_spmd} | conditional | flops 5646843904 | bytes 23857780 | solution.py:153
  721.7 10.5 %collective-permute-done = f32[256,512]{1,0:T(8,128)} collective-permute-done((f32[256,512]{1,0:T(8,128)S(1)}, f32[256,512]{1,0:T(8,128)}, u32[]{:S(2)}, u32[]{:S(2)}) %collective-permute-start) | collective-permute-done | bytes 524320 | tf_op jit(solution)/shard_map/while/body/eval_jaxpr/ppermute | solution.py:16
  741.1 24.9 %collective-permute-start = (f32[256,512]{1,0:T(8,128)S(1)}, f32[256,512]{1,0:T(8,128)}, u32[]{:S(2)}, u32[]{:S(2)}) collective-permute-start(f32[256,512]{1,0:T(8,128)S(1)} %get-tuple-element.431), channel_id=1, source_target_pairs={{0,16},{16,32},{32,48},{48,64},{64,80},{80,96},{96,112},{1,17},{17... | collective-permute-start | bytes 1572872 | tf_op jit(solution)/shard_map/while/body/eval_jaxpr/ppermute | solution.py:16
  783.7 6.0 collective-permute-start
  789.7 26.7 %collective-permute-start.1 = (f32[512,256]{1,0:T(8,128)S(1)}, f32[512,256]{1,0:T(8,128)}, u32[]{:S(2)}, u32[]{:S(2)}) collective-permute-start(f32[512,256]{1,0:T(8,128)S(1)} %get-tuple-element.432), channel_id=1, source_target_pairs={{0,16},{16,32},{32,48},{48,64},{64,80},{80,96},{96,112},{1,17},{17... | collective-permute-start | bytes 1572872 | tf_op jit(solution)/shard_map/while/body/eval_jaxpr/ppermute | solution.py:16
  826.3 7.2 collective-permute-start
  833.5 6.9 collective-permute-start.1
  849.4 26.2 %collective-permute-start.5 = (bf16[2,512,256]{2,1,0:T(8,128)(2,1)}, bf16[2,512,256]{2,1,0:T(8,128)(2,1)S(1)}, u32[]{:S(2)}, u32[]{:S(2)}) collective-permute-start(bf16[2,512,256]{2,1,0:T(8,128)(2,1)} %collective-permute-done.4), channel_id=1, source_target_pairs={{0,16},{16,32},{32,48},{48,64},{64,80},{80,96},{96,112},{1,17},{17... | collective-permute-start | bytes 1572872 | tf_op jit(solution)/shard_map/ppermute | solution.py:16
  887.2 6.2 fusion.82
  893.4 8.2 fusion.71
  901.6 6.6 convolution_convert_fusion
  908.2 100.9 %reduce-scatter.2.cloned.1.call-done = bf16[1024,256]{1,0:T(8,128)(2,1)} async-done(((bf16[1024,4096]{1,0:T(8,128)(2,1)}), bf16[1024,256]{1,0:T(8,128)(2,1)}) %reduce-scatter.2.cloned.1.call-update) | async-done | bytes 524304 | tf_op jit(solution)/shard_map/reduce_scatter | solution.py:166
  (205 shorter events, 294.0 us)
Async XLA Ops:
  6.5 895.0 %copy-start = (bf16[1,256,4096]{2,1,0:T(8,128)(2,1)S(1)}, bf16[1,256,4096]{2,1,0:T(8,128)(2,1)}, u32[]{:S(2)}) copy-start(bf16[1,256,4096]{2,1,0:T(8,128)(2,1)} %param.19) | copy-start | bytes 6291460
  6.5 65.2 %all-gather.2.cloned.1.call-start = ((), (), s32[]{:S(2)}) async-start(), calls=%async_computation.1 | async-start | bytes 8912896 | tf_op jit(solution)/shard_map/all_gather | solution.py:111
  7.3 1001.9 %reduce-scatter.2.cloned.1.call-start = ((), (), s32[]{:S(2)}) async-start(), calls=%async_computation.2 | async-start | bytes 8912896 | tf_op jit(solution)/shard_map/reduce_scatter | solution.py:166
  86.7 19.0 %collective-permute-start.6 = (bf16[2,512,256]{2,1,0:T(8,128)(2,1)S(1)}, bf16[2,512,256]{2,1,0:T(8,128)(2,1)S(1)}, u32[]{:S(2)}, u32[]{:S(2)}) collective-permute-start(bf16[2,512,256]{2,1,0:T(8,128)(2,1)S(1)} %bitcast.70), channel_id=1, source_target_pairs={{0,16},{16,32},{32,48},{48,64},{64,80},{80,96},{96,112},{1,17},{17... | collective-permute-start | bytes 1572872 | tf_op jit(solution)/shard_map/ppermute | solution.py:16
  93.1 23.8 %collective-permute-start.2 = (bf16[2,512,256]{2,1,0:T(8,128)(2,1)}, bf16[2,512,256]{2,1,0:T(8,128)(2,1)S(1)}, u32[]{:S(2)}, u32[]{:S(2)}) collective-permute-start(bf16[2,512,256]{2,1,0:T(8,128)(2,1)} %bitcast.8), channel_id=1, source_target_pairs={{0,16},{16,32},{32,48},{48,64},{64,80},{80,96},{96,112},{1,17},{17... | collective-permute-start | bytes 1572872 | tf_op jit(solution)/shard_map/ppermute | solution.py:16
  105.7 49.8 %copy-start.6 = (bf16[2,512,256]{2,1,0:T(8,128)(2,1)}, bf16[2,512,256]{2,1,0:T(8,128)(2,1)S(1)}, u32[]{:S(2)}) copy-start(bf16[2,512,256]{2,1,0:T(8,128)(2,1)S(1)} %collective-permute-done.6) | copy-start | bytes 1572868
  105.7 22.6 %collective-permute-start.7 = (bf16[2,512,256]{2,1,0:T(8,128)(2,1)S(1)}, bf16[2,512,256]{2,1,0:T(8,128)(2,1)}, u32[]{:S(2)}, u32[]{:S(2)}) collective-permute-start(bf16[2,512,256]{2,1,0:T(8,128)(2,1)S(1)} %collective-permute-done.6), channel_id=1, source_target_pairs={{0,16},{16,32},{32,48},{48,64},{64,80},{80,96},{96,112},{1,17},{17... | collective-permute-start | bytes 1572872 | tf_op jit(solution)/shard_map/ppermute | solution.py:16
  116.9 38.6 %copy-start.8 = (bf16[2,512,256]{2,1,0:T(8,128)(2,1)}, bf16[2,512,256]{2,1,0:T(8,128)(2,1)S(1)}, u32[]{:S(2)}) copy-start(bf16[2,512,256]{2,1,0:T(8,128)(2,1)S(1)} %collective-permute-done.2) | copy-start | bytes 1572868
  116.9 22.6 %collective-permute-start.3 = (bf16[2,512,256]{2,1,0:T(8,128)(2,1)S(1)}, bf16[2,512,256]{2,1,0:T(8,128)(2,1)}, u32[]{:S(2)}, u32[]{:S(2)}) collective-permute-start(bf16[2,512,256]{2,1,0:T(8,128)(2,1)S(1)} %collective-permute-done.2), channel_id=1, source_target_pairs={{0,16},{16,32},{32,48},{48,64},{64,80},{80,96},{96,112},{1,17},{17... | collective-permute-start | bytes 1572872 | tf_op jit(solution)/shard_map/ppermute | solution.py:16
  128.3 22.5 %collective-permute-start.8 = (bf16[2,512,256]{2,1,0:T(8,128)(2,1)}, bf16[2,512,256]{2,1,0:T(8,128)(2,1)}, u32[]{:S(2)}, u32[]{:S(2)}) collective-permute-start(bf16[2,512,256]{2,1,0:T(8,128)(2,1)} %collective-permute-done.7), channel_id=1, source_target_pairs={{0,16},{16,32},{32,48},{48,64},{64,80},{80,96},{96,112},{1,17},{17... | collective-permute-start | bytes 1572872 | tf_op jit(solution)/shard_map/ppermute | solution.py:16
  139.5 709.9 %collective-permute-start.4 = (bf16[2,512,256]{2,1,0:T(8,128)(2,1)}, bf16[2,512,256]{2,1,0:T(8,128)(2,1)}, u32[]{:S(2)}, u32[]{:S(2)}) collective-permute-start(bf16[2,512,256]{2,1,0:T(8,128)(2,1)} %collective-permute-done.3), channel_id=1, source_target_pairs={{0,16},{16,32},{32,48},{48,64},{64,80},{80,96},{96,112},{1,17},{17... | collective-permute-start | bytes 1572872 | tf_op jit(solution)/shard_map/ppermute | solution.py:16
  150.8 724.8 %collective-permute-start.9 = (bf16[2,512,256]{2,1,0:T(8,128)(2,1)}, bf16[2,512,256]{2,1,0:T(8,128)(2,1)}, u32[]{:S(2)}, u32[]{:S(2)}) collective-permute-start(bf16[2,512,256]{2,1,0:T(8,128)(2,1)} %collective-permute-done.8), channel_id=1, source_target_pairs={{0,16},{16,32},{32,48},{48,64},{64,80},{80,96},{96,112},{1,17},{17... | collective-permute-start | bytes 1572872 | tf_op jit(solution)/shard_map/ppermute | solution.py:16
  158.7 25.7 %collective-permute-start = (f32[256,512]{1,0:T(8,128)S(1)}, f32[256,512]{1,0:T(8,128)}, u32[]{:S(2)}, u32[]{:S(2)}) collective-permute-start(f32[256,512]{1,0:T(8,128)S(1)} %get-tuple-element.431), channel_id=1, source_target_pairs={{0,16},{16,32},{32,48},{48,64},{64,80},{80,96},{96,112},{1,17},{17... | collective-permute-start | bytes 1572872 | tf_op jit(solution)/shard_map/while/body/eval_jaxpr/ppermute | solution.py:16
  163.1 31.9 %collective-permute-start.1 = (f32[512,256]{1,0:T(8,128)S(1)}, f32[512,256]{1,0:T(8,128)}, u32[]{:S(2)}, u32[]{:S(2)}) collective-permute-start(f32[512,256]{1,0:T(8,128)S(1)} %get-tuple-element.432), channel_id=1, source_target_pairs={{0,16},{16,32},{32,48},{48,64},{64,80},{80,96},{96,112},{1,17},{17... | collective-permute-start | bytes 1572872 | tf_op jit(solution)/shard_map/while/body/eval_jaxpr/ppermute | solution.py:16
  198.2 19.3 %collective-permute-start = (f32[256,512]{1,0:T(8,128)S(1)}, f32[256,512]{1,0:T(8,128)}, u32[]{:S(2)}, u32[]{:S(2)}) collective-permute-start(f32[256,512]{1,0:T(8,128)S(1)} %get-tuple-element.431), channel_id=1, source_target_pairs={{0,16},{16,32},{32,48},{48,64},{64,80},{80,96},{96,112},{1,17},{17... | collective-permute-start | bytes 1572872 | tf_op jit(solution)/shard_map/while/body/eval_jaxpr/ppermute | solution.py:16
  201.8 25.3 %collective-permute-start.1 = (f32[512,256]{1,0:T(8,128)S(1)}, f32[512,256]{1,0:T(8,128)}, u32[]{:S(2)}, u32[]{:S(2)}) collective-permute-start(f32[512,256]{1,0:T(8,128)S(1)} %get-tuple-element.432), channel_id=1, source_target_pairs={{0,16},{16,32},{32,48},{48,64},{64,80},{80,96},{96,112},{1,17},{17... | collective-permute-start | bytes 1572872 | tf_op jit(solution)/shard_map/while/body/eval_jaxpr/ppermute | solution.py:16
  230.3 19.3 %collective-permute-start = (f32[256,512]{1,0:T(8,128)S(1)}, f32[256,512]{1,0:T(8,128)}, u32[]{:S(2)}, u32[]{:S(2)}) collective-permute-start(f32[256,512]{1,0:T(8,128)S(1)} %get-tuple-element.431), channel_id=1, source_target_pairs={{0,16},{16,32},{32,48},{48,64},{64,80},{80,96},{96,112},{1,17},{17... | collective-permute-start | bytes 1572872 | tf_op jit(solution)/shard_map/while/body/eval_jaxpr/ppermute | solution.py:16
  232.9 25.3 %collective-permute-start.1 = (f32[512,256]{1,0:T(8,128)S(1)}, f32[512,256]{1,0:T(8,128)}, u32[]{:S(2)}, u32[]{:S(2)}) collective-permute-start(f32[512,256]{1,0:T(8,128)S(1)} %get-tuple-element.432), channel_id=1, source_target_pairs={{0,16},{16,32},{32,48},{48,64},{64,80},{80,96},{96,112},{1,17},{17... | collective-permute-start | bytes 1572872 | tf_op jit(solution)/shard_map/while/body/eval_jaxpr/ppermute | solution.py:16
  261.4 92.8 %collective-permute-start = (f32[256,512]{1,0:T(8,128)S(1)}, f32[256,512]{1,0:T(8,128)}, u32[]{:S(2)}, u32[]{:S(2)}) collective-permute-start(f32[256,512]{1,0:T(8,128)S(1)} %get-tuple-element.431), channel_id=1, source_target_pairs={{0,16},{16,32},{32,48},{48,64},{64,80},{80,96},{96,112},{1,17},{17... | collective-permute-start | bytes 1572872 | tf_op jit(solution)/shard_map/while/body/eval_jaxpr/ppermute | solution.py:16
  263.3 97.9 %collective-permute-start.1 = (f32[512,256]{1,0:T(8,128)S(1)}, f32[512,256]{1,0:T(8,128)}, u32[]{:S(2)}, u32[]{:S(2)}) collective-permute-start(f32[512,256]{1,0:T(8,128)S(1)} %get-tuple-element.432), channel_id=1, source_target_pairs={{0,16},{16,32},{32,48},{48,64},{64,80},{80,96},{96,112},{1,17},{17... | collective-permute-start | bytes 1572872 | tf_op jit(solution)/shard_map/while/body/eval_jaxpr/ppermute | solution.py:16
  388.1 19.3 %collective-permute-start = (f32[256,512]{1,0:T(8,128)S(1)}, f32[256,512]{1,0:T(8,128)}, u32[]{:S(2)}, u32[]{:S(2)}) collective-permute-start(f32[256,512]{1,0:T(8,128)S(1)} %get-tuple-element.431), channel_id=1, source_target_pairs={{0,16},{16,32},{32,48},{48,64},{64,80},{80,96},{96,112},{1,17},{17... | collective-permute-start | bytes 1572872 | tf_op jit(solution)/shard_map/while/body/eval_jaxpr/ppermute | solution.py:16
  390.0 23.5 %collective-permute-start.1 = (f32[512,256]{1,0:T(8,128)S(1)}, f32[512,256]{1,0:T(8,128)}, u32[]{:S(2)}, u32[]{:S(2)}) collective-permute-start(f32[512,256]{1,0:T(8,128)S(1)} %get-tuple-element.432), channel_id=1, source_target_pairs={{0,16},{16,32},{32,48},{48,64},{64,80},{80,96},{96,112},{1,17},{17... | collective-permute-start | bytes 1572872 | tf_op jit(solution)/shard_map/while/body/eval_jaxpr/ppermute | solution.py:16
  416.6 37.1 %collective-permute-start = (f32[256,512]{1,0:T(8,128)S(1)}, f32[256,512]{1,0:T(8,128)}, u32[]{:S(2)}, u32[]{:S(2)}) collective-permute-start(f32[256,512]{1,0:T(8,128)S(1)} %get-tuple-element.431), channel_id=1, source_target_pairs={{0,16},{16,32},{32,48},{48,64},{64,80},{80,96},{96,112},{1,17},{17... | collective-permute-start | bytes 1572872 | tf_op jit(solution)/shard_map/while/body/eval_jaxpr/ppermute | solution.py:16
  441.5 17.8 %collective-permute-start.1 = (f32[512,256]{1,0:T(8,128)S(1)}, f32[512,256]{1,0:T(8,128)}, u32[]{:S(2)}, u32[]{:S(2)}) collective-permute-start(f32[512,256]{1,0:T(8,128)S(1)} %get-tuple-element.432), channel_id=1, source_target_pairs={{0,16},{16,32},{32,48},{48,64},{64,80},{80,96},{96,112},{1,17},{17... | collective-permute-start | bytes 1572872 | tf_op jit(solution)/shard_map/while/body/eval_jaxpr/ppermute | solution.py:16
  462.5 34.7 %collective-permute-start = (f32[256,512]{1,0:T(8,128)S(1)}, f32[256,512]{1,0:T(8,128)}, u32[]{:S(2)}, u32[]{:S(2)}) collective-permute-start(f32[256,512]{1,0:T(8,128)S(1)} %get-tuple-element.431), channel_id=1, source_target_pairs={{0,16},{16,32},{32,48},{48,64},{64,80},{80,96},{96,112},{1,17},{17... | collective-permute-start | bytes 1572872 | tf_op jit(solution)/shard_map/while/body/eval_jaxpr/ppermute | solution.py:16
  468.5 33.4 %collective-permute-start.1 = (f32[512,256]{1,0:T(8,128)S(1)}, f32[512,256]{1,0:T(8,128)}, u32[]{:S(2)}, u32[]{:S(2)}) collective-permute-start(f32[512,256]{1,0:T(8,128)S(1)} %get-tuple-element.432), channel_id=1, source_target_pairs={{0,16},{16,32},{32,48},{48,64},{64,80},{80,96},{96,112},{1,17},{17... | collective-permute-start | bytes 1572872 | tf_op jit(solution)/shard_map/while/body/eval_jaxpr/ppermute | solution.py:16
  505.1 22.2 %collective-permute-start = (f32[256,512]{1,0:T(8,128)S(1)}, f32[256,512]{1,0:T(8,128)}, u32[]{:S(2)}, u32[]{:S(2)}) collective-permute-start(f32[256,512]{1,0:T(8,128)S(1)} %get-tuple-element.431), channel_id=1, source_target_pairs={{0,16},{16,32},{32,48},{48,64},{64,80},{80,96},{96,112},{1,17},{17... | collective-permute-start | bytes 1572872 | tf_op jit(solution)/shard_map/while/body/eval_jaxpr/ppermute | solution.py:16
  515.6 17.3 %collective-permute-start.1 = (f32[512,256]{1,0:T(8,128)S(1)}, f32[512,256]{1,0:T(8,128)}, u32[]{:S(2)}, u32[]{:S(2)}) collective-permute-start(f32[512,256]{1,0:T(8,128)S(1)} %get-tuple-element.432), channel_id=1, source_target_pairs={{0,16},{16,32},{32,48},{48,64},{64,80},{80,96},{96,112},{1,17},{17... | collective-permute-start | bytes 1572872 | tf_op jit(solution)/shard_map/while/body/eval_jaxpr/ppermute | solution.py:16
  536.1 33.0 %collective-permute-start = (f32[256,512]{1,0:T(8,128)S(1)}, f32[256,512]{1,0:T(8,128)}, u32[]{:S(2)}, u32[]{:S(2)}) collective-permute-start(f32[256,512]{1,0:T(8,128)S(1)} %get-tuple-element.431), channel_id=1, source_target_pairs={{0,16},{16,32},{32,48},{48,64},{64,80},{80,96},{96,112},{1,17},{17... | collective-permute-start | bytes 1572872 | tf_op jit(solution)/shard_map/while/body/eval_jaxpr/ppermute | solution.py:16
  557.3 17.9 %collective-permute-start.1 = (f32[512,256]{1,0:T(8,128)S(1)}, f32[512,256]{1,0:T(8,128)}, u32[]{:S(2)}, u32[]{:S(2)}) collective-permute-start(f32[512,256]{1,0:T(8,128)S(1)} %get-tuple-element.432), channel_id=1, source_target_pairs={{0,16},{16,32},{32,48},{48,64},{64,80},{80,96},{96,112},{1,17},{17... | collective-permute-start | bytes 1572872 | tf_op jit(solution)/shard_map/while/body/eval_jaxpr/ppermute | solution.py:16
  578.4 19.3 %collective-permute-start = (f32[256,512]{1,0:T(8,128)S(1)}, f32[256,512]{1,0:T(8,128)}, u32[]{:S(2)}, u32[]{:S(2)}) collective-permute-start(f32[256,512]{1,0:T(8,128)S(1)} %get-tuple-element.431), channel_id=1, source_target_pairs={{0,16},{16,32},{32,48},{48,64},{64,80},{80,96},{96,112},{1,17},{17... | collective-permute-start | bytes 1572872 | tf_op jit(solution)/shard_map/while/body/eval_jaxpr/ppermute | solution.py:16
  586.1 17.6 %collective-permute-start.1 = (f32[512,256]{1,0:T(8,128)S(1)}, f32[512,256]{1,0:T(8,128)}, u32[]{:S(2)}, u32[]{:S(2)}) collective-permute-start(f32[512,256]{1,0:T(8,128)S(1)} %get-tuple-element.432), channel_id=1, source_target_pairs={{0,16},{16,32},{32,48},{48,64},{64,80},{80,96},{96,112},{1,17},{17... | collective-permute-start | bytes 1572872 | tf_op jit(solution)/shard_map/while/body/eval_jaxpr/ppermute | solution.py:16
  606.8 18.7 %collective-permute-start = (f32[256,512]{1,0:T(8,128)S(1)}, f32[256,512]{1,0:T(8,128)}, u32[]{:S(2)}, u32[]{:S(2)}) collective-permute-start(f32[256,512]{1,0:T(8,128)S(1)} %get-tuple-element.431), channel_id=1, source_target_pairs={{0,16},{16,32},{32,48},{48,64},{64,80},{80,96},{96,112},{1,17},{17... | collective-permute-start | bytes 1572872 | tf_op jit(solution)/shard_map/while/body/eval_jaxpr/ppermute | solution.py:16
  611.9 19.2 %collective-permute-start.1 = (f32[512,256]{1,0:T(8,128)S(1)}, f32[512,256]{1,0:T(8,128)}, u32[]{:S(2)}, u32[]{:S(2)}) collective-permute-start(f32[512,256]{1,0:T(8,128)S(1)} %get-tuple-element.432), channel_id=1, source_target_pairs={{0,16},{16,32},{32,48},{48,64},{64,80},{80,96},{96,112},{1,17},{17... | collective-permute-start | bytes 1572872 | tf_op jit(solution)/shard_map/while/body/eval_jaxpr/ppermute | solution.py:16
  634.3 49.1 %collective-permute-start = (f32[256,512]{1,0:T(8,128)S(1)}, f32[256,512]{1,0:T(8,128)}, u32[]{:S(2)}, u32[]{:S(2)}) collective-permute-start(f32[256,512]{1,0:T(8,128)S(1)} %get-tuple-element.431), channel_id=1, source_target_pairs={{0,16},{16,32},{32,48},{48,64},{64,80},{80,96},{96,112},{1,17},{17... | collective-permute-start | bytes 1572872 | tf_op jit(solution)/shard_map/while/body/eval_jaxpr/ppermute | solution.py:16
  636.9 52.2 %collective-permute-start.1 = (f32[512,256]{1,0:T(8,128)S(1)}, f32[512,256]{1,0:T(8,128)}, u32[]{:S(2)}, u32[]{:S(2)}) collective-permute-start(f32[512,256]{1,0:T(8,128)S(1)} %get-tuple-element.432), channel_id=1, source_target_pairs={{0,16},{16,32},{32,48},{48,64},{64,80},{80,96},{96,112},{1,17},{17... | collective-permute-start | bytes 1572872 | tf_op jit(solution)/shard_map/while/body/eval_jaxpr/ppermute | solution.py:16
  715.8 16.4 %collective-permute-start = (f32[256,512]{1,0:T(8,128)S(1)}, f32[256,512]{1,0:T(8,128)}, u32[]{:S(2)}, u32[]{:S(2)}) collective-permute-start(f32[256,512]{1,0:T(8,128)S(1)} %get-tuple-element.431), channel_id=1, source_target_pairs={{0,16},{16,32},{32,48},{48,64},{64,80},{80,96},{96,112},{1,17},{17... | collective-permute-start | bytes 1572872 | tf_op jit(solution)/shard_map/while/body/eval_jaxpr/ppermute | solution.py:16
  717.8 20.1 %collective-permute-start.1 = (f32[512,256]{1,0:T(8,128)S(1)}, f32[512,256]{1,0:T(8,128)}, u32[]{:S(2)}, u32[]{:S(2)}) collective-permute-start(f32[512,256]{1,0:T(8,128)S(1)} %get-tuple-element.432), channel_id=1, source_target_pairs={{0,16},{16,32},{32,48},{48,64},{64,80},{80,96},{96,112},{1,17},{17... | collective-permute-start | bytes 1572872 | tf_op jit(solution)/shard_map/while/body/eval_jaxpr/ppermute | solution.py:16
  741.1 33.8 %collective-permute-start = (f32[256,512]{1,0:T(8,128)S(1)}, f32[256,512]{1,0:T(8,128)}, u32[]{:S(2)}, u32[]{:S(2)}) collective-permute-start(f32[256,512]{1,0:T(8,128)S(1)} %get-tuple-element.431), channel_id=1, source_target_pairs={{0,16},{16,32},{32,48},{48,64},{64,80},{80,96},{96,112},{1,17},{17... | collective-permute-start | bytes 1572872 | tf_op jit(solution)/shard_map/while/body/eval_jaxpr/ppermute | solution.py:16
  766.0 14.5 %collective-permute-start.1 = (f32[512,256]{1,0:T(8,128)S(1)}, f32[512,256]{1,0:T(8,128)}, u32[]{:S(2)}, u32[]{:S(2)}) collective-permute-start(f32[512,256]{1,0:T(8,128)S(1)} %get-tuple-element.432), channel_id=1, source_target_pairs={{0,16},{16,32},{32,48},{48,64},{64,80},{80,96},{96,112},{1,17},{17... | collective-permute-start | bytes 1572872 | tf_op jit(solution)/shard_map/while/body/eval_jaxpr/ppermute | solution.py:16
  783.7 34.6 %collective-permute-start = (f32[256,512]{1,0:T(8,128)S(1)}, f32[256,512]{1,0:T(8,128)}, u32[]{:S(2)}, u32[]{:S(2)}) collective-permute-start(f32[256,512]{1,0:T(8,128)S(1)} %get-tuple-element.431), channel_id=1, source_target_pairs={{0,16},{16,32},{32,48},{48,64},{64,80},{80,96},{96,112},{1,17},{17... | collective-permute-start | bytes 1572872 | tf_op jit(solution)/shard_map/while/body/eval_jaxpr/ppermute | solution.py:16
  789.7 33.4 %collective-permute-start.1 = (f32[512,256]{1,0:T(8,128)S(1)}, f32[512,256]{1,0:T(8,128)}, u32[]{:S(2)}, u32[]{:S(2)}) collective-permute-start(f32[512,256]{1,0:T(8,128)S(1)} %get-tuple-element.432), channel_id=1, source_target_pairs={{0,16},{16,32},{32,48},{48,64},{64,80},{80,96},{96,112},{1,17},{17... | collective-permute-start | bytes 1572872 | tf_op jit(solution)/shard_map/while/body/eval_jaxpr/ppermute | solution.py:16
  826.3 16.0 %collective-permute-start = (f32[256,512]{1,0:T(8,128)S(1)}, f32[256,512]{1,0:T(8,128)}, u32[]{:S(2)}, u32[]{:S(2)}) collective-permute-start(f32[256,512]{1,0:T(8,128)S(1)} %get-tuple-element.431), channel_id=1, source_target_pairs={{0,16},{16,32},{32,48},{48,64},{64,80},{80,96},{96,112},{1,17},{17... | collective-permute-start | bytes 1572872 | tf_op jit(solution)/shard_map/while/body/eval_jaxpr/ppermute | solution.py:16
  833.5 14.4 %collective-permute-start.1 = (f32[512,256]{1,0:T(8,128)S(1)}, f32[512,256]{1,0:T(8,128)}, u32[]{:S(2)}, u32[]{:S(2)}) collective-permute-start(f32[512,256]{1,0:T(8,128)S(1)} %get-tuple-element.432), channel_id=1, source_target_pairs={{0,16},{16,32},{32,48},{48,64},{64,80},{80,96},{96,112},{1,17},{17... | collective-permute-start | bytes 1572872 | tf_op jit(solution)/shard_map/while/body/eval_jaxpr/ppermute | solution.py:16
  847.8 31.0 %copy-start.7 = (bf16[2,512,256]{2,1,0:T(8,128)(2,1)S(1)}, bf16[2,512,256]{2,1,0:T(8,128)(2,1)}, u32[]{:S(2)}) copy-start(bf16[2,512,256]{2,1,0:T(8,128)(2,1)} %copy-done.6) | copy-start | bytes 1572868
  847.8 31.0 %copy-start.5 = (bf16[1024,256]{1,0:T(8,128)(2,1)S(1)}, bf16[1024,256]{1,0:T(8,128)(2,1)}, u32[]{:S(2)}) copy-start(bf16[1024,256]{1,0:T(8,128)(2,1)} %copy-done.4) | copy-start | bytes 1572868
  849.4 32.9 %collective-permute-start.5 = (bf16[2,512,256]{2,1,0:T(8,128)(2,1)}, bf16[2,512,256]{2,1,0:T(8,128)(2,1)S(1)}, u32[]{:S(2)}, u32[]{:S(2)}) collective-permute-start(bf16[2,512,256]{2,1,0:T(8,128)(2,1)} %collective-permute-done.4), channel_id=1, source_target_pairs={{0,16},{16,32},{32,48},{48,64},{64,80},{80,96},{96,112},{1,17},{17... | collective-permute-start | bytes 1572872 | tf_op jit(solution)/shard_map/ppermute | solution.py:16
  878.9 6.7 copy-start.10
  (8 other events, 37.3 us)
Sparse Core Ops, SparseCore 0:
  9.0 62.7 all-gather.1
  908.3 100.7 reduce-scatter.1
where the time goes:
time: 1020 us
  waiting for transfers between devices  511 us (50%)
  starting transfers between devices  306 us (30%)
  matrix products  81.7 us (8%)
  other arithmetic  72.8 us (7%)
  local copies, waits for them, and re-layouts  25.6 us (3%)
  between operations  14.3 us (1%)
    ppermute x40, waiting for transfers between devices, shifted(): return lax.ppermute(block, axis, route)  345 us
    ppermute x40, starting transfers between devices, shifted(): return lax.ppermute(block, axis, route)  306 us
    reduce_scatter x1, waiting for transfers between devices, body(): lax.psum_scatter(partial_value.astype(jnp.bfloat16), 'head', scatter_dime...  101 us
    all_gather x1, waiting for transfers between devices, body(): piece = lax.all_gather(flattened, 'head', axis=1, tiled=True)  64.5 us
    select_n x16, other arithmetic, turn(): fast_all = jnp.where(live, stored, fast_all)  31 us
  transfers between devices with their start and end apart: 42, of which 36 were waited for; matrix products, arithmetic and copies ran while one was open for 14% of the time, Pallas kernels for 0%

commit v1 on v0

v1 whole, which is shorter than its diff:
```python
import functools
import jax
import jax.numpy as jnp
from jax import lax
from jax.experimental import pallas as pl
from jax.experimental.pallas import tpu as pltpu
from jax.sharding import PartitionSpec as P

WIN = 2048
NS_STEPS = 3
UPDATE_RATE = 0.3
LOG2E = 1.4426950408889634
MESH = pl.DeviceIdType.MESH
NT = (((1,), (1,)), ((), ()))
TN = (((0,), (0,)), ((), ()))
NN = (((1,), (0,)), ((), ()))


def mm(a, b, dims=NN):
    return lax.dot_general(a, b, dims, preferred_element_type=jnp.float32)


def half(a):
    return a.astype(jnp.bfloat16)


def sigmoid(a):
    return 0.5 * jnp.tanh(0.5 * a) + 0.5


def unit_scaled(update):
    return update * lax.rsqrt(jnp.sum(update * update) + 1e-06)


def chain_step(state_a, state_b, k, g):
    hidden = mm(k, half(state_a[...]))
    back = mm(g, half(state_b[...]))
    gate = sigmoid(hidden)
    act = half(hidden * gate)
    slopes = half(back * gate * (1.0 + hidden * (1.0 - gate)))
    xa = unit_scaled(mm(k, slopes, TN))
    xb = unit_scaled(mm(g, act, TN))
    for _ in range(NS_STEPS):
        ha, hb = half(xa), half(xb)
        gram_a = half(mm(ha, ha, NT))
        gram_b = half(mm(hb, hb, NT))
        xa = 1.5 * xa - 0.5 * mm(gram_a, ha)
        xb = 1.5 * xb - 0.5 * mm(gram_b, hb)
    state_a[...] += UPDATE_RATE * xa
    state_b[...] += UPDATE_RATE * xb


def column_kernel(
    length, reach,
    scale_ref, gain_ref, q_ref, k_ref, v_ref, g_ref, a0_ref, b0_ref, out_ref,
    kwin, vwin, ck, cg, sent_a, sent_b, got_a, got_b, state_a, state_b, top, total, acc,
    feed_send, feed_k, feed_g, own_sem, win_send, win_k, win_v, w_send, w_recv,
):
    p = lax.axis_index("seq")
    h = lax.axis_index("head")
    core = lax.rem(h, 2)
    owners = (core, 3 - core)
    seqs, group, width = q_ref.shape

    barrier = pltpu.get_barrier_semaphore()
    for d in range(1, length):
        pl.semaphore_signal(
            barrier, inc=1, device_id=(lax.rem(p + d, length), h), device_id_type=MESH
        )
    pl.semaphore_wait(barrier, length - 1)

    def feed(s, which):
        src, dst, sem = ((k_ref, ck, feed_k), (g_ref, cg, feed_g))[which]
        return pltpu.make_async_remote_copy(
            src_ref=src.at[s], dst_ref=dst.at[p],
            send_sem=feed_send.at[s, which], recv_sem=sem.at[p],
            device_id=(owners[s], h), device_id_type=MESH,
        )

    def keep(s, which):
        src, dst = ((k_ref, ck), (g_ref, cg))[which]
        return pltpu.make_async_copy(src.at[s], dst.at[p], own_sem.at[which])

    for s in range(seqs):
        for which in range(2):
            pl.when(p != owners[s])(feed(s, which).start)
            pl.when(p == owners[s])(keep(s, which).start)

    def window(d, which):
        src, dst, sem = ((k_ref, kwin, win_k), (v_ref, vwin, win_v))[which]
        return pltpu.make_async_remote_copy(
            src_ref=src, dst_ref=dst.at[d - 1],
            send_sem=win_send.at[d - 1, which], recv_sem=sem.at[d - 1],
            device_id=(lax.rem(p + d, length), h), device_id_type=MESH,
        )

    for d in range(1, reach + 1):
        for which in range(2):
            pl.when(p + d < length)(window(d, which).start)

    def weights(s, b, which):
        src, dst = ((sent_a, got_a), (sent_b, got_b))[which]
        return pltpu.make_async_remote_copy(
            src_ref=src.at[b], dst_ref=dst.at[s],
            send_sem=w_send.at[which, b], recv_sem=w_recv.at[which, s],
            device_id=(b, h), device_id_type=MESH,
        )

    def chain(s):
        state_a[...] = a0_ref[...]
        state_b[...] = b0_ref[...]

        def turn(b, carry):
            @pl.when(b != p)
            def _():
                for dst, sem in ((ck, feed_k), (cg, feed_g)):
                    pltpu.make_async_remote_copy(
                        src_ref=dst.at[b], dst_ref=dst.at[b],
                        send_sem=feed_send.at[0, 0], recv_sem=sem.at[b],
                        device_id=(b, h), device_id_type=MESH,
                    ).wait_recv()

            @pl.when(b == p)
            def _():
                for which in range(2):
                    keep(s, which).wait()

            chain_step(state_a, state_b, ck[b], cg[b])
            new_a, new_b = half(state_a[...]), half(state_b[...])

            @pl.when(b != p)
            def _():
                sent_a[b] = new_a
                weights(s, b, 0).start()
                sent_b[b] = new_b
                weights(s, b, 1).start()

            @pl.when(b == p)
            def _():
                got_a[s] = new_a
                got_b[s] = new_b

            return carry

        lax.fori_loop(0, length, turn, 0)

    for s in range(seqs):
        pl.when(p == owners[s])(functools.partial(chain, s))

    sharp = scale_ref[0] * LOG2E
    tile = group // 2

    def scores(s, r, keys):
        rows = pl.ds(pl.multiple_of(r * tile, tile), tile)
        return rows, mm(q_ref[s, rows], keys, NT) * sharp

    def first(i, carry):
        s, r = i // 2, i % 2
        rows, sc = scores(s, r, k_ref[s])
        row = lax.broadcasted_iota(jnp.int32, sc.shape, 0) + r * tile
        col = lax.broadcasted_iota(jnp.int32, sc.shape, 1)
        sc = jnp.where(col <= row, sc, -1e30)
        high = jnp.max(sc, axis=1, keepdims=True)
        w = jnp.exp2(sc - high)
        top[s, rows] = high
        total[s, rows] = jnp.sum(w, axis=1, keepdims=True)
        acc[s, rows] = mm(half(w), v_ref[s])
        return carry

    lax.fori_loop(0, 2 * seqs, first, 0)

    def later(d, i, carry):
        s, r = i // 2, i % 2
        rows, sc = scores(s, r, kwin[d - 1, s])
        if d == reach:
            row = lax.broadcasted_iota(jnp.int32, sc.shape, 0) + r * tile
            col = lax.broadcasted_iota(jnp.int32, sc.shape, 1)
            sc = jnp.where(col >= row, sc, -1e30)
        old = top[s, rows]
        high = jnp.maximum(old, jnp.max(sc, axis=1, keepdims=True))
        w = jnp.exp2(sc - high)
        shrink = jnp.exp2(old - high)
        top[s, rows] = high
        total[s, rows] = total[s, rows] * shrink + jnp.sum(w, axis=1, keepdims=True)
        acc[s, rows] = acc[s, rows] * shrink + mm(half(w), vwin[d - 1, s])
        return carry

    for d in range(1, reach + 1):

        @pl.when(p >= d)
        def _():
            for which in range(2):
                window(d, which).wait_recv()
            lax.fori_loop(0, 2 * seqs, functools.partial(later, d), 0)

    for s in range(seqs):

        @pl.when(p != owners[s])
        def _():
            weights(s, p, 0).wait_recv()

        hidden = mm(q_ref[s], got_a[s])
        act = half(hidden * sigmoid(hidden))

        @pl.when(p != owners[s])
        def _():
            weights(s, p, 1).wait_recv()

        fast = mm(act, got_b[s], NT)
        fast = fast * lax.rsqrt(jnp.mean(fast * fast, axis=1, keepdims=True) + 1e-05)
        out_ref[s] = half(acc[s] / total[s] + fast * gain_ref[...])

    for s in range(seqs):
        for which in range(2):
            pl.when(p != owners[s])(feed(s, which).wait_send)
    for d in range(1, reach + 1):
        for which in range(2):
            pl.when(p + d < length)(window(d, which).wait_send)

    @pl.when((p == owners[0]) | (p == owners[1]))
    def _():
        def done(b, carry):
            @pl.when(b != p)
            def _():
                for which in range(2):
                    weights(0, b, which).wait_send()

            return carry

        lax.fori_loop(0, length, done, 0)


def column(scale, gain, q, k, v, g, a0, b0, collective_id):
    seqs, group, width = q.shape
    hid = a0.shape[1]
    length = lax.axis_size("seq")
    reach = WIN // group
    vmem = pl.BlockSpec(memory_space=pltpu.VMEM)
    dma = pltpu.SemaphoreType.DMA
    bf16, f32 = jnp.bfloat16, jnp.float32
    return pl.pallas_call(
        functools.partial(column_kernel, length, reach),
        out_shape=jax.ShapeDtypeStruct(q.shape, bf16),
        in_specs=[pl.BlockSpec(memory_space=pltpu.SMEM)] + [vmem] * 7,
        out_specs=vmem,
        scratch_shapes=[
            pltpu.VMEM((reach, seqs, group, width), bf16),
            pltpu.VMEM((reach, seqs, group, width), bf16),
            pltpu.VMEM((length, group, width), bf16),
            pltpu.VMEM((length, group, width), bf16),
            pltpu.VMEM((length, width, hid), bf16),
            pltpu.VMEM((length, width, hid), bf16),
            pltpu.VMEM((seqs, width, hid), bf16),
            pltpu.VMEM((seqs, width, hid), bf16),
            pltpu.VMEM((width, hid), f32),
            pltpu.VMEM((width, hid), f32),
            pltpu.VMEM((seqs, group, 1), f32),
            pltpu.VMEM((seqs, group, 1), f32),
            pltpu.VMEM((seqs, group, width), f32),
            dma((seqs, 2)), dma((length,)), dma((length,)), dma((2,)),
            dma((reach, 2)), dma((reach,)), dma((reach,)),
            dma((2, length)), dma((2, seqs)),
        ],
        compiler_params=pltpu.CompilerParams(
            collective_id=collective_id, has_side_effects=True, vmem_limit_bytes=48 << 20
        ),
        cost_estimate=pl.CostEstimate(
            flops=10**10, bytes_accessed=10**7, transcendentals=10**6
        ),
    )(scale, gain, q, k, v, g, a0, b0)


def prepare(projected, rate_col, count_seqs):
    head_dim = projected.shape[1] // 3
    query_rows = projected[:, :head_dim]
    keys = projected[:, head_dim : 2 * head_dim]
    values = projected[:, 2 * head_dim :]
    query_norm = (
        query_rows * lax.rsqrt(jnp.sum(query_rows * query_rows, axis=1, keepdims=True) + 1e-06)
    ).astype(jnp.bfloat16)
    key_norm = (keys * lax.rsqrt(jnp.sum(keys * keys, axis=1, keepdims=True) + 1e-06)).astype(
        jnp.bfloat16
    )
    value_half = values.astype(jnp.bfloat16)
    weighted = (jax.nn.softplus(rate_col) * values).astype(jnp.bfloat16)
    return tuple(
        a.reshape(count_seqs, -1, head_dim) for a in (query_norm, key_norm, value_half, weighted)
    )


def body(x, w_in, w_rate, scale, gain, a0, b0, w_out):
    seqs, group, local = x.shape
    rows = seqs * group
    flat = x.reshape(rows, local)
    w_in = w_in.reshape(w_in.shape[0], w_in.shape[2])
    piece = lax.all_gather(flat, "head", axis=1, tiled=True)
    projected = jnp.dot(piece, w_in, preferred_element_type=jnp.float32)
    rate_col = jnp.dot(piece, w_rate, preferred_element_type=jnp.float32)
    q, k, v, g = prepare(projected, rate_col, seqs)
    head_out = column(scale, gain, q, k, v, g, a0[0], b0[0].T, 1)
    head_out = head_out.reshape(rows, -1)
    partial = jnp.dot(head_out, w_out[0], preferred_element_type=jnp.float32)
    result = lax.psum_scatter(
        partial.astype(jnp.bfloat16), "head", scatter_dimension=1, tiled=True
    )
    return result.reshape(seqs, group, -1)


def solution(mesh):
    in_specs = (
        P(None, "seq", "head"),
        P(None, "head", None),
        P(None, "head"),
        P("head"),
        P("head", None),
        P("head", None, None),
        P("head", None, None),
        P("head", None, None),
    )
    out_specs = P(None, "seq", "head")
    return jax.shard_map(body, mesh=mesh, in_specs=in_specs, out_specs=out_specs, check_vma=False)
```

time: 1020 us -> 331 us (0.32)
  waiting for transfers between devices: 511 us -> 189 us
  starting transfers between devices: 306 us -> 0.04 us
  Pallas kernels: 0 us -> 104 us
  other arithmetic: 72.8 us -> 0.85 us
  matrix products: 81.7 us -> 18.9 us
  local copies, waits for them, and re-layouts: 25.6 us -> 1.32 us
    ppermute x40 -> x0, waiting for transfers between devices: 345 us -> none  [shifted(): return lax.ppermute(block, axis, route)]
    ppermute x40 -> x0, starting transfers between devices: 306 us -> none  [shifted(): return lax.ppermute(block, axis, route)]
    pallas_call x0 -> x1, Pallas kernels: none -> 104 us  [column(): pl.pallas_call(functools.partial(column_kernel, length, reach), out_shape...]
    select_n x48 -> x0, other arithmetic: 66.9 us -> none  [the longest x16 31 us: turn(): fast_all = jnp.where(live, stored, fast_all)]
    dot_general x36 -> x3, matrix products: 75.5 us -> 18.9 us  [the longest x1 11 us: body(): projected = jnp.dot(piece, w_in, preferred_element_type=jnp.float32)]
    reduce_scatter x1, waiting for transfers between devices: 101 us -> 125 us  [body(): lax.psum_scatter(partial.astype(jnp.bfloat16), 'head', scatter_dimension=...]
    broadcast_in_dim x15 -> x0, local copies, waits for them, and re-layouts: 13.7 us -> none  [the longest x14 12.7 us: turn(): stored = lax.dynamic_update_index_in_dim(fast_all, fast, which, 0)]
  transfers between devices with their start and end apart: 42 -> 2, of which waited for: 36 -> 2; matrix products, arithmetic and copies ran while one was open for 14% -> 0% of each run, Pallas kernels for 0% -> 0%
where the time goes in v1:
time: 331 us; the launch traced here: 328 us
  waiting for transfers between devices  189 us (57%)
  Pallas kernels  104 us (31%)
  matrix products  18.9 us (6%)
  between operations  14.2 us (4%)
    reduce_scatter x1, waiting for transfers between devices, body(): lax.psum_scatter(partial.astype(jnp.bfloat16), 'head', scatter_dimension=...  125 us
    pallas_call x1, Pallas kernels, column(): pl.pallas_call(functools.partial(column_kernel, length, reach), out_shape...  104 us
    all_gather x1, waiting for transfers between devices, body(): piece = lax.all_gather(flat, 'head', axis=1, tiled=True)  62.6 us
    dot_general x1, matrix products, body(): projected = jnp.dot(piece, w_in, preferred_element_type=jnp.float32)  11 us
  transfers between devices with their start and end apart: 2, of which 2 were waited for; matrix products, arithmetic and copies ran while one was open for 0% of the time, Pallas kernels for 0%

profile of v1, /device:TPU:16, one launch (start us, length us, event | category | flops | bytes accessed | tf_op | source)
XLA Modules:
  0.0 327.9 jit_solution(6362011200201283910)
XLA Ops:
  6.5 0.0 copy-start
  6.5 0.0 all-gather.2.cloned.1.call-start
  6.5 0.7 all-gather.2.cloned.1.call-update
  7.3 0.0 reduce-scatter.2.cloned.1.call-start
  8.0 1.2 copy.9
  9.2 0.0 copy-start.4
  9.2 62.6 %all-gather.2.cloned.1.call-done = bf16[1024,4096]{1,0:T(8,128)(2,1)} async-done(((bf16[1024,256]{1,0:T(8,128)(2,1)}), bf16[1024,4096]{1,0:T(8,128)(2,1)}) %all-gather.2.cloned.1.call-update) | async-done | bytes 8388624 | tf_op jit(solution)/shard_map/all_gather | solution.py:296
  71.8 0.0 copy-start.3
  71.8 11.0 %fusion = f32[1024,768]{1,0:T(8,128)S(1)} fusion(bf16[1024,4096]{1,0:T(8,128)(2,1)} %all-gather.2.cloned.1.call-done, bf16[4096,1,768]{2,0,1:T(8,128)(2,1)} %param.9), kind=kOutput, calls=%fused_computation.1 | convolution fusion | flops 6442450944 | bytes 17825792 | tf_op jit(solution)/shard_map/dot_general | solution.py:297
  82.8 0.3 multiply_reduce_fusion
  83.2 0.1 slice.21
  83.2 0.0 copy-done.4
  83.2 0.0 copy-done.3
  83.2 0.0 copy-start.1
  83.3 0.0 copy-start.2
  83.3 2.3 fusion.3
  85.6 0.5 multiply_convert_fusion
  86.1 0.0 copy-done.1
  86.1 0.0 copy-done.2
  86.1 104.0 %shard_map.82 = bf16[2,512,256]{2,1,0:T(8,128)(2,1)S(1)} custom-call(f32[1]{0:T(128)S(6)} %copy.10.scale_ref, f32[1,256]{1,0:T(1,128)S(1)} %copy-done.2, bf16[2,512,256]{2,1,0:T(8,128)(2,1)S(1)} %bitcast.26, bf16[2,512,256]{2,1,0:T(8,128)(2,1)S(1)} %bitcast.25, bf16[2,512,256]{2,1,0:T(8,128)(2,1)S(1)} %bitcast.23, bf16[2,512,256]{2,1,0:T(8,128)(2,1)S(1)} %bitcast.24, ...), custom_call_target="tpu_custom_call" | custom-call | flops 10000000000 | bytes 10000000 | tf_op jit(solution)/shard_map/pallas_call | solution.py:241
  190.1 0.0 copy-done
  190.1 5.6 %convolution_convert_fusion = bf16[1024,4096]{1,0:T(8,128)(2,1)} fusion(bf16[1024,256]{1,0:T(8,128)(2,1)S(1)} %bitcast.27, bf16[1,256,4096]{2,1,0:T(8,128)(2,1)S(1)} %copy-done), kind=kOutput, calls=%fused_computation | convolution fusion | flops 2151677952 | bytes 11010048 | tf_op jit(solution)/shard_map/dot_general | solution.py:302
  195.7 0.0 reduce-scatter.2.cloned.1.call-update
  195.7 125.3 %reduce-scatter.2.cloned.1.call-done = bf16[1024,256]{1,0:T(8,128)(2,1)} async-done(((bf16[1024,4096]{1,0:T(8,128)(2,1)}), bf16[1024,256]{1,0:T(8,128)(2,1)}) %reduce-scatter.2.cloned.1.call-update) | async-done | bytes 524304 | tf_op jit(solution)/shard_map/reduce_scatter | solution.py:303
  (2 shorter events, 0.0 us)
Async XLA Ops:
  6.5 183.6 %copy-start = (bf16[1,256,4096]{2,1,0:T(8,128)(2,1)S(1)}, bf16[1,256,4096]{2,1,0:T(8,128)(2,1)}, u32[]{:S(2)}) copy-start(bf16[1,256,4096]{2,1,0:T(8,128)(2,1)} %param.15) | copy-start | bytes 6291460
  6.5 65.2 %all-gather.2.cloned.1.call-start = ((), (), s32[]{:S(2)}) async-start(), calls=%async_computation.1 | async-start | bytes 8912896 | tf_op jit(solution)/shard_map/all_gather | solution.py:296
  7.3 313.8 %reduce-scatter.2.cloned.1.call-start = ((), (), s32[]{:S(2)}) async-start(), calls=%async_computation.2 | async-start | bytes 8912896 | tf_op jit(solution)/shard_map/reduce_scatter | solution.py:303
  9.2 74.0 %copy-start.4 = (bf16[4096,1]{0,1:T(2,128)(2,1)S(1)}, bf16[4096,1]{0,1:T(2,128)(2,1)}, u32[]{:S(2)}) copy-start(bf16[4096,1]{0,1:T(2,128)(2,1)} %param.10) | copy-start | bytes 24580
  71.8 11.5 %copy-start.3 = (bf16[1024,4096]{1,0:T(8,128)(2,1)S(1)}, bf16[1024,4096]{1,0:T(8,128)(2,1)}, u32[]{:S(2)}) copy-start(bf16[1024,4096]{1,0:T(8,128)(2,1)} %all-gather.2.cloned.1.call-done) | copy-start | bytes 25165828
  83.2 2.8 copy-start.1
  83.3 2.8 copy-start.2
Sparse Core Ops, SparseCore 0:
  9.0 62.7 all-gather.1
  195.8 125.1 reduce-scatter.1

commit v2 on v1

--- a/solution.py
+++ b/solution.py
@@ -270,40 +270,194 @@
     )(scale, gain, q, k, v, g, a0, b0)
 
 
-def prepare(projected, rate_col, count_seqs):
-    head_dim = projected.shape[1] // 3
-    query_rows = projected[:, :head_dim]
-    keys = projected[:, head_dim : 2 * head_dim]
-    values = projected[:, 2 * head_dim :]
-    query_norm = (
-        query_rows * lax.rsqrt(jnp.sum(query_rows * query_rows, axis=1, keepdims=True) + 1e-06)
-    ).astype(jnp.bfloat16)
-    key_norm = (keys * lax.rsqrt(jnp.sum(keys * keys, axis=1, keepdims=True) + 1e-06)).astype(
-        jnp.bfloat16
-    )
-    value_half = values.astype(jnp.bfloat16)
-    weighted = (jax.nn.softplus(rate_col) * values).astype(jnp.bfloat16)
-    return tuple(
-        a.reshape(count_seqs, -1, head_dim) for a in (query_norm, key_norm, value_half, weighted)
-    )
+def gather_kernel(
+    finish, n_out, *refs,
+):
+    x_ref, w_hbm = refs[0], refs[1]
+    extra = refs[2:-8 - n_out]
+    outs = refs[-8 - n_out:-8]
+    held, weights, acc, side, w_sem, send_sem, recv_sem, spare = refs[-8:]
+    seq = lax.axis_index("seq")
+    me = lax.axis_index("head")
+    x, z, core = me // 4, (me // 2) % 2, me % 2
+
+    def at(dx, dz, dc):
+        return ((x + dx + 4) % 4) * 4 + ((z + dz) % 2) * 2 + (core + dc) % 2
+
+    plus, minus, across, twin = at(1, 0, 0), at(-1, 0, 0), at(0, 1, 0), at(0, 0, 1)
+
+    load = pltpu.make_async_copy(w_hbm, weights, w_sem)
+    load.start()
+
+    barrier = pltpu.get_barrier_semaphore()
+    for other in (plus, minus, across, twin):
+        pl.semaphore_signal(barrier, inc=1, device_id=(seq, other), device_id_type=MESH)
+    pl.semaphore_wait(barrier, 4)
+
+    sends = []
+
+    def send(chunk, t, target, own=False):
+        copy = pltpu.make_async_remote_copy(
+            src_ref=x_ref.at[t] if own else held.at[chunk, t],
+            dst_ref=held.at[chunk, t],
+            send_sem=send_sem.at[len(sends)],
+            recv_sem=recv_sem.at[chunk, t],
+            device_id=(seq, target), device_id_type=MESH,
+        )
+        copy.start()
+        sends.append(copy)
+
+    def arrived(chunk, t):
+        pltpu.make_async_remote_copy(
+            src_ref=held.at[chunk, t], dst_ref=held.at[chunk, t],
+            send_sem=send_sem.at[0], recv_sem=recv_sem.at[chunk, t],
+            device_id=(seq, twin), device_id_type=MESH,
+        ).wait_recv()
+
+    for i in range(2):
+        send(me, i, plus, True)
+        send(me, 1 - i, minus, True)
+        send(me, i, across, True)
+    for i in range(2):
+        send(me, i, twin, True)
+
+    finish.init(extra, acc, side)
+    load.wait()
+
+    def use(chunk, own=False):
+        def step(t, carry):
+            block = x_ref[t] if own else held[chunk, t]
+            acc[t] += mm(block, weights[chunk])
+            finish.each(extra, side, t, chunk, block)
+            return carry
+
+        lax.fori_loop(0, 2, step, 0)
+
+    def take(dx, dz, t, targets):
+        chunk = at(dx, dz, 0)
+        arrived(chunk, t)
+        for target in targets:
+            send(chunk, t, target)
+        send(chunk, t, twin)
+
+    def pair(dx, dz):
+        chunk = at(dx, dz, 1)
+        for t in range(2):
+            arrived(chunk, t)
+        use(chunk)
+
+    use(me, True)
+    take(-1, 0, 0, (plus,))
+    take(1, 0, 1, (minus,))
+    take(0, 1, 0, (plus, minus))
+    pair(0, 0)
+    take(-1, 0, 1, ())
+    take(1, 0, 0, ())
+    take(0, 1, 1, (plus, minus))
+    use(at(-1, 0, 0))
+    use(at(1, 0, 0))
+    use(at(0, 1, 0))
+    pair(-1, 0)
+    pair(1, 0)
+    pair(0, 1)
+    take(2, 0, 0, (across,))
+    take(2, 0, 1, (across,))
+    use(at(2, 0, 0))
+    pair(2, 0)
+    take(-1, 1, 0, ())
+    take(1, 1, 0, ())
+    take(2, 1, 0, ())
+    take(-1, 1, 1, ())
+    take(1, 1, 1, ())
+    use(at(-1, 1, 0))
+    use(at(1, 1, 0))
+    take(2, 1, 1, ())
+    use(at(2, 1, 0))
+    pair(-1, 1)
+    pair(1, 1)
+    pair(2, 1)
+    finish.last(extra, acc, side, outs)
+    for copy in sends:
+        copy.wait_send()
+
+
+class Projection:
+    def init(extra, acc, side):
+        acc[...] = jnp.zeros_like(acc)
+        side[...] = jnp.zeros_like(side)
+
+    def each(extra, side, t, chunk, block):
+        rate = extra[0][chunk]
+        lanes = side.shape[2]
+        wide = block.astype(jnp.float32)
+        total = wide[:, :lanes] * rate[:, :lanes]
+        for at in range(lanes, block.shape[1], lanes):
+            total += wide[:, at:at + lanes] * rate[:, at:at + lanes]
+        side[t] += total
+
+    def last(extra, acc, side, outs):
+        width = acc.shape[2] // 3
+        for t in range(2):
+            q, k, v = (acc[t, :, i * width:(i + 1) * width] for i in range(3))
+            rate = jnp.sum(side[t], axis=1, keepdims=True)
+            step = jnp.maximum(rate, 0.0) + jnp.log1p(jnp.exp(-jnp.abs(rate)))
+            outs[0][t] = half(q * lax.rsqrt(jnp.sum(q * q, axis=1, keepdims=True) + 1e-06))
+            outs[1][t] = half(k * lax.rsqrt(jnp.sum(k * k, axis=1, keepdims=True) + 1e-06))
+            outs[2][t] = half(v)
+            outs[3][t] = half(step * v)
+
+
+class Mixing:
+    def init(extra, acc, side):
+        acc[...] = jnp.zeros_like(acc)
+
+    def each(extra, side, t, chunk, block):
+        pass
+
+    def last(extra, acc, side, outs):
+        outs[0][...] = half(acc[...])
+
+
+def gather_matmul(x, w, extra, finish, n_out, collective_id):
+    seqs, group, local = x.shape
+    ways = lax.axis_size("head")
+    wide = w.shape[2]
+    vmem = pl.BlockSpec(memory_space=pltpu.VMEM)
+    dma = pltpu.SemaphoreType.DMA
+    out = jax.ShapeDtypeStruct((seqs, group, 256), jnp.bfloat16)
+    return pl.pallas_call(
+        functools.partial(gather_kernel, finish, n_out),
+        out_shape=[out] * n_out,
+        in_specs=[vmem, pl.BlockSpec(memory_space=pl.ANY)] + [vmem] * len(extra),
+        out_specs=[vmem] * n_out,
+        scratch_shapes=[
+            pltpu.VMEM((ways, seqs, group, local), jnp.bfloat16),
+            pltpu.VMEM(w.shape, jnp.bfloat16),
+            pltpu.VMEM((seqs, group, wide), jnp.float32),
+            pltpu.VMEM((seqs, group, 128), jnp.float32),
+            dma, dma((32,)), dma((ways, 2)), dma,
+        ],
+        compiler_params=pltpu.CompilerParams(
+            collective_id=collective_id, has_side_effects=True, vmem_limit_bytes=40 << 20
+        ),
+        cost_estimate=pl.CostEstimate(
+            flops=2 * seqs * group * ways * local * wide, bytes_accessed=10**7, transcendentals=0
+        ),
+    )(x, w, *extra)
 
 
 def body(x, w_in, w_rate, scale, gain, a0, b0, w_out):
-    seqs, group, local = x.shape
-    rows = seqs * group
-    flat = x.reshape(rows, local)
-    w_in = w_in.reshape(w_in.shape[0], w_in.shape[2])
-    piece = lax.all_gather(flat, "head", axis=1, tiled=True)
-    projected = jnp.dot(piece, w_in, preferred_element_type=jnp.float32)
-    rate_col = jnp.dot(piece, w_rate, preferred_element_type=jnp.float32)
-    q, k, v, g = prepare(projected, rate_col, seqs)
+    ways = lax.axis_size("head")
+    local = x.shape[2]
+    w_in = w_in.reshape(ways, local, w_in.shape[2])
+    rate = w_rate.astype(jnp.float32).reshape(ways, 1, local)
+    pieces = w_out[0].reshape(-1, ways, local).transpose(1, 0, 2)
+    q, k, v, g = gather_matmul(x, w_in, (rate,), Projection, 4, 2)
+    pieces, q = lax.optimization_barrier((pieces, q))
+    mixing = lax.all_to_all(pieces, "head", split_axis=0, concat_axis=0, tiled=True)
     head_out = column(scale, gain, q, k, v, g, a0[0], b0[0].T, 1)
-    head_out = head_out.reshape(rows, -1)
-    partial = jnp.dot(head_out, w_out[0], preferred_element_type=jnp.float32)
-    result = lax.psum_scatter(
-        partial.astype(jnp.bfloat16), "head", scatter_dimension=1, tiled=True
-    )
-    return result.reshape(seqs, group, -1)
+    (out,) = gather_matmul(head_out, mixing, (), Mixing, 1, 3)
+    return out
 
 
 def solution(mesh):

time: 331 us -> 248 us (0.75)
  waiting for transfers between devices: 189 us -> 0.01 us
  Pallas kernels: 104 us -> 219 us
  matrix products: 18.9 us -> 0 us
  local copies, waits for them, and re-layouts: 1.32 us -> 19.7 us
  between operations: 14.2 us -> 0.78 us
  starting transfers between devices: 0.04 us -> 4.16 us
    reduce_scatter x1 -> x0, waiting for transfers between devices: 125 us -> none  [body(): lax.psum_scatter(partial.astype(jnp.bfloat16), 'head', scatter_dimension=...]
    pallas_call x0 -> x2, Pallas kernels: none -> 101 us  [gather_matmul(): pl.pallas_call(functools.partial(gather_kernel, finish, n_out), out_shape...]
    all_gather x1 -> x0, waiting for transfers between devices: 62.6 us -> none  [body(): piece = lax.all_gather(flat, 'head', axis=1, tiled=True)]
    dot_general x3 -> x0, matrix products: 18.9 us -> none  [the longest x1 11 us: body(): projected = jnp.dot(piece, w_in, preferred_element_type=jnp.float32)]
    unnamed x11 -> x33, local copies, waits for them, and re-layouts: 1.26 us -> 17.3 us
    pallas_call x1, Pallas kernels: 104 us -> 119 us  [column(): pl.pallas_call(functools.partial(column_kernel, length, reach), out_shape...]
    all_to_all x0 -> x1, starting transfers between devices: none -> 4.16 us  [body(): lax.all_to_all(pieces, 'head', split_axis=0, concat_axis=0, tiled=True)]
  transfers between devices with their start and end apart: 2 -> 1, of which waited for: 2 -> 0; matrix products, arithmetic and copies ran while one was open for 0% -> 1% of each run, Pallas kernels for 0% -> 49%
where the time goes in v2:
time: 248 us; the launch traced here: 244 us
  Pallas kernels  219 us (88%)
  local copies, waits for them, and re-layouts  19.7 us (8%)
  starting transfers between devices  4.16 us (2%)
    pallas_call x1, Pallas kernels, column(): pl.pallas_call(functools.partial(column_kernel, length, reach), out_shape...  119 us
    pallas_call x2, Pallas kernels, gather_matmul(): pl.pallas_call(functools.partial(gather_kernel, finish, n_out), out_shape...  101 us
    unnamed x33, local copies, waits for them, and re-layouts  17.3 us
  transfers between devices with their start and end apart: 1, of which 0 were waited for; matrix products, arithmetic and copies ran while one was open for 1% of the time, Pallas kernels for 49%

profile of v2, /device:TPU:16, one launch (start us, length us, event | category | flops | bytes accessed | tf_op | source)
XLA Modules:
  0.0 243.8 jit_solution(3471228961771012103)
XLA Ops:
  0.0 3.3 %copy.10 = bf16[1,256,4096]{1,2,0:T(8,128)(2,1)S(1)} copy(bf16[1,256,4096]{2,1,0:T(8,128)(2,1)} %param.15) | data formatting | bytes 4194304 | tf_op args[7]
  3.3 0.0 copy-start.14
  3.3 0.0 copy-start.1
  3.3 2.4 copy.11
  5.7 0.0 copy-done.14
  5.7 0.0 copy-done.1
  5.8 0.0 copy-start
  5.8 2.8 %copy-done = bf16[4096,1,768]{2,0,1:T(8,128)(2,1)S(1)} copy-done((bf16[4096,1,768]{2,0,1:T(8,128)(2,1)S(1)}, bf16[4096,1,768]{2,0,1:T(8,128)(2,1)}, u32[]{:S(2)}) %copy-start) | copy-done | bytes 6291480
  8.5 39.4 %shard_map.82 = (bf16[2,512,256]{2,1,0:T(8,128)(2,1)S(1)}, bf16[2,512,256]{2,1,0:T(8,128)(2,1)S(1)}, bf16[2,512,256]{2,1,0:T(8,128)(2,1)S(1)}, bf16[2,512,256]{2,1,0:T(8,128)(2,1)S(1)}) custom-call(bf16[2,512,256]{2,1,0:T(8,128)(2,1)S(1)} %copy-done.1, bf16[16,256,768]{2,1,0:T(8,128)(2,1)S(1)} %bitcast.10, f32[16,1,256]{2,1,0:T(1,128)S(1)} %convert.1.refs_2_), custom_call_target="tpu_custom_call" | custom-call | flops 6442450944 | bytes 10000000 | tf_op jit(solution)/shard_map/pallas_call | solution.py:428
  48.0 0.0 copy-start.6
  48.0 0.8 copy-done.6
  48.8 0.0 copy-start.8
  48.8 0.8 copy-done.8
  49.6 0.0 copy-start.10
  49.6 0.8 copy-done.10
  50.4 0.0 copy-start.12
  50.4 0.8 copy-done.12
  51.2 0.0 copy-start.2
  51.2 0.0 copy-start.3
  51.2 4.2 %all-to-all-start = ((bf16[16,256,256]{2,1,0:T(8,128)(2,1)}), bf16[16,256,256]{2,1,0:T(8,128)(2,1)S(1)}, u32[]{:S(2)}, u32[]{:S(2)}) async-start(bf16[16,256,256]{2,1,0:T(8,128)(2,1)} %bitcast.12), calls=%async_computation | async-start | bytes 4194304 | tf_op jit(solution)/shard_map/all_to_all | solution.py:457
  56.0 1.2 copy.12
  57.3 0.0 copy-done.2
  57.3 0.0 copy-done.3
  57.3 0.0 copy-start.7
  57.3 1.0 copy-done.7
  58.3 0.0 copy-start.9
  58.3 1.0 copy-done.9
  59.4 0.0 copy-start.11
  59.4 1.0 copy-done.11
  60.4 0.0 copy-start.13
  60.4 1.0 copy-done.13
  61.5 118.5 %shard_map.83.refs_0_ = bf16[2,512,256]{2,1,0:T(8,128)(2,1)S(1)} custom-call(f32[1]{0:T(128)S(6)} %copy.14.scale_ref, f32[1,256]{1,0:T(1,128)S(1)} %copy-done.3, bf16[2,512,256]{2,1,0:T(8,128)(2,1)S(1)} %copy-done.7, bf16[2,512,256]{2,1,0:T(8,128)(2,1)S(1)} %copy-done.9, bf16[2,512,256]{2,1,0:T(8,128)(2,1)S(1)} %copy-done.11, ...), custom_call_target="tpu_custom_call" | custom-call | flops 10000000000 | bytes 10000000 | tf_op jit(solution)/shard_map/pallas_call | solution.py:241
  180.0 0.0 copy-start.4
  180.0 0.8 copy-done.4
  180.8 0.0 all-to-all-done.refs_1_
  180.8 0.0 copy-start.5
  180.8 1.0 copy-done.5
  181.8 61.1 %shard_map.84 = bf16[2,512,256]{2,1,0:T(8,128)(2,1)S(1)} custom-call(bf16[2,512,256]{2,1,0:T(8,128)(2,1)S(1)} %copy-done.5, bf16[16,256,256]{2,1,0:T(8,128)(2,1)S(1)} %all-to-all-done.refs_1_), custom_call_target="tpu_custom_call" | custom-call | flops 2147483648 | bytes 10000000 | tf_op jit(solution)/shard_map/pallas_call | solution.py:428
  243.0 0.8 copy.15
  (1 shorter events, 0.0 us)
Async XLA Ops:
  3.3 2.4 %copy-start.14 = (bf16[4096,1]{0,1:T(2,128)(2,1)S(1)}, bf16[4096,1]{0,1:T(2,128)(2,1)}, u32[]{:S(2)}) copy-start(bf16[4096,1]{0,1:T(2,128)(2,1)} %param.10) | copy-start | bytes 24580
  3.3 2.5 %copy-start.1 = (bf16[2,512,256]{2,1,0:T(8,128)(2,1)S(1)}, bf16[2,512,256]{2,1,0:T(8,128)(2,1)}, u32[]{:S(2)}) copy-start(bf16[2,512,256]{2,1,0:T(8,128)(2,1)} %refs_0_.1) | copy-start | bytes 1572868
  5.8 2.8 %copy-start = (bf16[4096,1,768]{2,0,1:T(8,128)(2,1)S(1)}, bf16[4096,1,768]{2,0,1:T(8,128)(2,1)}, u32[]{:S(2)}) copy-start(bf16[4096,1,768]{2,0,1:T(8,128)(2,1)} %param.9) | copy-start | bytes 18874372
  48.0 0.8 copy-start.6
  48.8 0.8 copy-start.8
  49.6 0.8 copy-start.10
  50.4 0.8 copy-start.12
  51.2 6.1 %copy-start.2 = (f32[1,256,512]{2,1,0:T(8,128)S(1)}, f32[1,256,512]{2,1,0:T(8,128)}, u32[]{:S(2)}) copy-start(f32[1,256,512]{2,1,0:T(8,128)} %param.13) | copy-start | bytes 1572868
  51.2 6.1 %copy-start.3 = (f32[1,256]{1,0:T(1,128)S(1)}, f32[1,256]{1,0:T(1,128)}, u32[]{:S(2)}) copy-start(f32[1,256]{1,0:T(1,128)} %gain_ref.1) | copy-start | bytes 3076
  51.2 129.6 %all-to-all-start = ((bf16[16,256,256]{2,1,0:T(8,128)(2,1)}), bf16[16,256,256]{2,1,0:T(8,128)(2,1)S(1)}, u32[]{:S(2)}, u32[]{:S(2)}) async-start(bf16[16,256,256]{2,1,0:T(8,128)(2,1)} %bitcast.12), calls=%async_computation | async-start | bytes 4194304 | tf_op jit(solution)/shard_map/all_to_all | solution.py:457
  57.3 1.0 copy-start.7
  58.3 1.0 copy-start.9
  59.4 1.0 copy-start.11
  60.4 1.0 copy-start.13
  180.0 0.8 copy-start.4
  180.8 1.0 copy-start.5

commit v3 on v2

v3 whole, which is shorter than its diff:
```python
import functools
import jax
import jax.numpy as jnp
from jax import lax
from jax.experimental import pallas as pl
from jax.experimental.pallas import tpu as pltpu
from jax.sharding import PartitionSpec as P

WIN = 2048
NS_STEPS = 3
UPDATE_RATE = 0.3
LOG2E = 1.4426950408889634
MESH = pl.DeviceIdType.MESH
NT = (((1,), (1,)), ((), ()))
TN = (((0,), (0,)), ((), ()))
NN = (((1,), (0,)), ((), ()))


def mm(a, b, dims=NN):
    return lax.dot_general(a, b, dims, preferred_element_type=jnp.float32)


def half(a):
    return a.astype(jnp.bfloat16)


def sigmoid(a):
    return 0.5 * jnp.tanh(0.5 * a) + 0.5


def unit_scaled(update):
    return update * lax.rsqrt(jnp.sum(update * update) + 1e-06)


def chain_step(state_a, state_b, k, g):
    hidden = mm(k, half(state_a[...]))
    back = mm(g, half(state_b[...]))
    gate = sigmoid(hidden)
    act = half(hidden * gate)
    slopes = half(back * gate * (1.0 + hidden * (1.0 - gate)))
    xa = unit_scaled(mm(k, slopes, TN))
    xb = unit_scaled(mm(g, act, TN))
    for _ in range(NS_STEPS):
        ha, hb = half(xa), half(xb)
        gram_a = half(mm(ha, ha, NT))
        gram_b = half(mm(hb, hb, NT))
        xa = 1.5 * xa - 0.5 * mm(gram_a, ha)
        xb = 1.5 * xb - 0.5 * mm(gram_b, hb)
    state_a[...] += UPDATE_RATE * xa
    state_b[...] += UPDATE_RATE * xb


def ring_of(p):
    return p // 2, p % 2


def column_kernel(
    far_owner, late_windows,
    scale_ref, gain_ref, q_ref, k_ref, v_ref, g_ref, a0_ref, b0_ref, w_ref, out_ref, mix_ref,
    kwin, vwin, ck, cg, sent_a, sent_b, got_a, got_b, state_a, state_b, top, total, acc,
    feed_send, feed_k, feed_g, own_sem, win_send, win_k, win_v, w_send, w_recv,
    mix_send, mix_recv, mix_own,
):
    p = lax.axis_index("seq")
    h = lax.axis_index("head")
    y, plane = ring_of(p)
    length = lax.axis_size("seq")
    ways = lax.axis_size("head")
    ring = length // 2
    owner = (h % 2) * far_owner
    pair, group, width = q_ref.shape
    reach = 2

    def place(row):
        return (row % ring) * 2 + plane

    barrier = pltpu.get_barrier_semaphore()
    for d in range(1, ring):
        pl.semaphore_signal(barrier, inc=1, device_id=(place(y + d), h), device_id_type=MESH)
    for d in range(1, ways):
        pl.semaphore_signal(barrier, inc=1, device_id=(p, (h + d) % ways), device_id_type=MESH)
    pl.semaphore_wait(barrier, ring + ways - 2)

    def feed(j, which):
        src, dst, sem = ((k_ref, ck, feed_k), (g_ref, cg, feed_g))[which]
        return pltpu.make_async_remote_copy(
            src_ref=src.at[j], dst_ref=dst.at[2 * y + j],
            send_sem=feed_send.at[j, which], recv_sem=sem.at[2 * y + j],
            device_id=(place(owner), h), device_id_type=MESH,
        )

    def keep(j, which):
        src, dst = ((k_ref, ck), (g_ref, cg))[which]
        return pltpu.make_async_copy(src.at[j], dst.at[2 * y + j], own_sem.at[j, which])

    for j in range(pair):
        for which in range(2):
            pl.when(y != owner)(feed(j, which).start)
            pl.when(y == owner)(keep(j, which).start)

    def window(d, which):
        src, dst, sem = ((k_ref, kwin, win_k), (v_ref, vwin, win_v))[which]
        return pltpu.make_async_remote_copy(
            src_ref=src, dst_ref=dst.at[d - 1],
            send_sem=win_send.at[d - 1, which], recv_sem=sem.at[d - 1],
            device_id=(place(y + d), h), device_id_type=MESH,
        )

    def windows():
        for d in range(1, reach + 1):
            for which in range(2):
                pl.when(y + d < ring)(window(d, which).start)

    def mixing(d):
        other = (h + d) % ways
        return pltpu.make_async_remote_copy(
            src_ref=w_ref.at[:, pl.ds(pl.multiple_of(other * width, width), width)],
            dst_ref=mix_ref.at[h],
            send_sem=mix_send.at[d], recv_sem=mix_recv.at[d],
            device_id=(p, other), device_id_type=MESH,
        )

    mine = pltpu.make_async_copy(
        w_ref.at[:, pl.ds(pl.multiple_of(h * width, width), width)], mix_ref.at[h], mix_own
    )

    if not late_windows:
        windows()
    mine.start()
    for d in range(1, ways):
        mixing(d).start()
    if late_windows:

        @pl.when(y != owner)
        def _():
            for j in range(pair):
                for which in range(2):
                    feed(j, which).wait_send()

        windows()

    def weights(b, which):
        src, dst = ((sent_a, got_a), (sent_b, got_b))[which]
        return pltpu.make_async_remote_copy(
            src_ref=src.at[b], dst_ref=dst.at[b % 2],
            send_sem=w_send.at[which, b], recv_sem=w_recv.at[which, b % 2],
            device_id=(place(b // 2), h), device_id_type=MESH,
        )

    @pl.when(y == owner)
    def _():
        state_a[...] = a0_ref[...]
        state_b[...] = b0_ref[...].T
        for j in range(pair):
            for which in range(2):
                keep(j, which).wait()

        def turn(b, carry):
            @pl.when(b // 2 != y)
            def _():
                for dst, sem in ((ck, feed_k), (cg, feed_g)):
                    pltpu.make_async_remote_copy(
                        src_ref=dst.at[b], dst_ref=dst.at[b],
                        send_sem=feed_send.at[0, 0], recv_sem=sem.at[b],
                        device_id=(place(y + 1), h), device_id_type=MESH,
                    ).wait_recv()

            chain_step(state_a, state_b, ck[b], cg[b])
            new_a, new_b = half(state_a[...]), half(state_b[...])

            @pl.when(b // 2 != y)
            def _():
                sent_a[b] = new_a
                weights(b, 0).start()
                sent_b[b] = new_b
                weights(b, 1).start()

            @pl.when(b // 2 == y)
            def _():
                got_a[b % 2] = new_a
                got_b[b % 2] = new_b

            return carry

        lax.fori_loop(0, length, turn, 0)

    sharp = scale_ref[0] * LOG2E
    tile = group // 2

    def score(j, r, keys, edge):
        rows = pl.ds(pl.multiple_of(r * tile, tile), tile)
        sc = mm(q_ref[j, rows], keys, NT) * sharp
        if edge:
            row = lax.broadcasted_iota(jnp.int32, sc.shape, 0) + r * tile
            col = lax.broadcasted_iota(jnp.int32, sc.shape, 1)
            sc = jnp.where((col <= row) if edge == 1 else (col >= row), sc, -1e30)
        return rows, sc

    def first(i, carry):
        j, r = i // 2, i % 2
        rows, sc = score(j, r, k_ref[j], 1)
        high = jnp.max(sc, axis=1, keepdims=True)
        w = jnp.exp2(sc - high)
        top[j, rows] = high
        total[j, rows] = jnp.sum(w, axis=1, keepdims=True)
        acc[j, rows] = mm(half(w), v_ref[j])
        return carry

    def fold(j, r, keys, values, edge):
        rows, sc = score(j, r, keys, edge)
        old = top[j, rows]
        high = jnp.maximum(old, jnp.max(sc, axis=1, keepdims=True))
        w = jnp.exp2(sc - high)
        shrink = jnp.exp2(old - high)
        top[j, rows] = high
        total[j, rows] = total[j, rows] * shrink + jnp.sum(w, axis=1, keepdims=True)
        acc[j, rows] = acc[j, rows] * shrink + mm(half(w), values)

    lax.fori_loop(0, 2 * pair, first, 0)

    def own(r, carry):
        fold(1, r, k_ref[0], v_ref[0], 0)
        return carry

    lax.fori_loop(0, 2, own, 0)

    @pl.when(y >= 1)
    def _():
        for which in range(2):
            window(1, which).wait_recv()

        def near(i, carry):
            b = i % 2
            fold(i // 4, (i // 2) % 2, kwin[0, b], vwin[0, b], 0)
            return carry

        lax.fori_loop(0, 8, near, 0)

    @pl.when(y >= 2)
    def _():
        for which in range(2):
            window(2, which).wait_recv()

        def edge(i, carry):
            j = i // 2
            fold(j, i % 2, kwin[1, j], vwin[1, j], 2)
            return carry

        lax.fori_loop(0, 4, edge, 0)

        def inner(r, carry):
            fold(0, r, kwin[1, 1], vwin[1, 1], 0)
            return carry

        lax.fori_loop(0, 2, inner, 0)

    for j in range(pair):

        @pl.when(y != owner)
        def _():
            weights(2 * y + j, 0).wait_recv()

        hidden = mm(q_ref[j], got_a[j])
        act = half(hidden * sigmoid(hidden))

        @pl.when(y != owner)
        def _():
            weights(2 * y + j, 1).wait_recv()

        fast = mm(act, got_b[j], NT)
        fast = fast * lax.rsqrt(jnp.mean(fast * fast, axis=1, keepdims=True) + 1e-05)
        out_ref[j] = half(acc[j] / total[j] + fast * gain_ref[...])

    if not late_windows:

        @pl.when(y != owner)
        def _():
            for j in range(pair):
                for which in range(2):
                    feed(j, which).wait_send()

    for d in range(1, reach + 1):
        for which in range(2):
            pl.when(y + d < ring)(window(d, which).wait_send)
    mine.wait()
    for d in range(1, ways):
        mixing(d).wait_send()
        pltpu.make_async_remote_copy(
            src_ref=mix_ref.at[(h - d + ways) % ways], dst_ref=mix_ref.at[(h - d + ways) % ways],
            send_sem=mix_send.at[d], recv_sem=mix_recv.at[d],
            device_id=(p, (h + d) % ways), device_id_type=MESH,
        ).wait_recv()

    @pl.when(y == owner)
    def _():
        def done(b, carry):
            @pl.when(b // 2 != y)
            def _():
                for which in range(2):
                    weights(b, which).wait_send()

            return carry

        lax.fori_loop(0, length, done, 0)


FAR_OWNER = 3
LATE_WINDOWS = False


def column(scale, gain, q, k, v, g, a0, b0, w_out, collective_id):
    pair, group, width = q.shape
    hid = a0.shape[1]
    length = lax.axis_size("seq")
    ways = lax.axis_size("head")
    vmem = pl.BlockSpec(memory_space=pltpu.VMEM)
    dma = pltpu.SemaphoreType.DMA
    bf16, f32 = jnp.bfloat16, jnp.float32
    return pl.pallas_call(
        functools.partial(column_kernel, FAR_OWNER, LATE_WINDOWS),
        out_shape=[
            jax.ShapeDtypeStruct(q.shape, bf16),
            jax.ShapeDtypeStruct((ways, width, width), bf16),
        ],
        in_specs=[pl.BlockSpec(memory_space=pltpu.SMEM)] + [vmem] * 7
        + [pl.BlockSpec(memory_space=pl.ANY)],
        out_specs=[vmem, vmem],
        scratch_shapes=[
            pltpu.VMEM((2, pair, group, width), bf16),
            pltpu.VMEM((2, pair, group, width), bf16),
            pltpu.VMEM((length, group, width), bf16),
            pltpu.VMEM((length, group, width), bf16),
            pltpu.VMEM((length, width, hid), bf16),
            pltpu.VMEM((length, width, hid), bf16),
            pltpu.VMEM((pair, width, hid), bf16),
            pltpu.VMEM((pair, width, hid), bf16),
            pltpu.VMEM((width, hid), f32),
            pltpu.VMEM((width, hid), f32),
            pltpu.VMEM((pair, group, 1), f32),
            pltpu.VMEM((pair, group, 1), f32),
            pltpu.VMEM((pair, group, width), f32),
            dma((pair, 2)), dma((length,)), dma((length,)), dma((pair, 2)),
            dma((2, 2)), dma((2,)), dma((2,)),
            dma((2, length)), dma((2, pair)),
            dma((ways,)), dma((ways,)), dma,
        ],
        compiler_params=pltpu.CompilerParams(
            collective_id=collective_id, has_side_effects=True, vmem_limit_bytes=48 << 20
        ),
        cost_estimate=pl.CostEstimate(
            flops=10**10, bytes_accessed=10**7, transcendentals=10**6
        ),
    )(scale, gain, q, k, v, g, a0, b0, w_out)


def gather_kernel(finish, n_in, n_out, *refs):
    x_ref, w_hbm = refs[:2]
    extra = refs[2:2 + n_in]
    outs = refs[2 + n_in:2 + n_in + n_out]
    held, weights, acc, side, stage, w_sem, send_sem, recv_sem, swap_sem = refs[2 + n_in + n_out:]
    p = lax.axis_index("seq")
    me = lax.axis_index("head")
    y, plane = ring_of(p)
    partner = 2 * y + 1 - plane
    x, z, core = me // 4, (me // 2) % 2, me % 2
    first = plane if finish.inward else 1 - plane

    def at(dx, dz, dc):
        return ((x + dx + 4) % 4) * 4 + ((z + dz) % 2) * 2 + (core + dc) % 2

    plus, minus, across, twin = at(1, 0, 0), at(-1, 0, 0), at(0, 1, 0), at(0, 0, 1)

    load = pltpu.make_async_copy(w_hbm, weights, w_sem)
    load.start()

    barrier = pltpu.get_barrier_semaphore()
    pl.semaphore_signal(barrier, inc=1, device_id=(partner, me), device_id_type=MESH)
    for other in (plus, minus, across, twin):
        pl.semaphore_signal(barrier, inc=1, device_id=(p, other), device_id_type=MESH)
    pl.semaphore_wait(barrier, 5)

    sends = []

    def send(chunk, t, target, source=None):
        copy = pltpu.make_async_remote_copy(
            src_ref=held.at[chunk, t] if source is None else source,
            dst_ref=held.at[chunk, t],
            send_sem=send_sem.at[len(sends)],
            recv_sem=recv_sem.at[chunk, t],
            device_id=target, device_id_type=MESH,
        )
        copy.start()
        sends.append(copy)

    def arrived(chunk, t):
        pltpu.make_async_remote_copy(
            src_ref=held.at[chunk, t], dst_ref=held.at[chunk, t],
            send_sem=send_sem.at[0], recv_sem=recv_sem.at[chunk, t],
            device_id=(p, twin), device_id_type=MESH,
        ).wait_recv()

    if finish.inward:
        send(me, 1, (partner, me), x_ref.at[1 - first])
    for other in (plus, minus, across, twin):
        send(me, 0, (p, other), x_ref.at[first])
    if not finish.inward:
        for other in (minus, plus, across, twin):
            send(me, 1, (p, other), x_ref.at[1 - first])
        held[me, 1] = x_ref[1 - first]
    held[me, 0] = x_ref[first]

    acc[...] = jnp.zeros_like(acc)
    finish.start(side)
    load.wait()

    def take(dx, dz, t, targets):
        chunk = at(dx, dz, 0)
        arrived(chunk, t)
        for target in targets:
            send(chunk, t, (p, target))
        send(chunk, t, (p, twin))

    def use(dx, dz, t):
        here, there = at(dx, dz, 0), at(dx, dz, 1)
        arrived(there, t)

        def step(i, carry):
            chunk = here + i * (there - here)
            block = held[chunk, t]
            acc[t] += mm(block, weights[chunk])
            finish.each(extra, side, t, chunk, block)
            return carry

        lax.fori_loop(0, 2, step, 0)

    take(-1, 0, 0, (plus,))
    take(0, 1, 0, (plus, minus))
    take(1, 0, 0, ())
    if finish.inward:
        arrived(me, 1)
        for other in (minus, plus, across, twin):
            send(me, 1, (p, other))
    use(0, 0, 0)
    use(-1, 0, 0)
    use(0, 1, 0)
    use(1, 0, 0)
    take(1, 0, 1, (minus,))
    take(0, 1, 1, (minus, plus))
    take(-1, 0, 1, ())
    take(2, 0, 0, (across,))
    use(0, 0, 1)
    use(2, 0, 0)
    take(-1, 1, 0, ())
    take(1, 1, 0, ())
    use(1, 0, 1)
    use(0, 1, 1)
    use(-1, 0, 1)
    take(2, 0, 1, (across,))
    take(2, 1, 0, ())
    use(-1, 1, 0)
    use(1, 1, 0)
    use(2, 1, 0)
    back = None
    if not finish.inward:
        stage[...] = half(acc[0])
        back = pltpu.make_async_remote_copy(
            src_ref=stage, dst_ref=outs[0].at[plane],
            send_sem=swap_sem.at[0], recv_sem=swap_sem.at[1],
            device_id=(partner, me), device_id_type=MESH,
        )
        back.start()
    use(2, 0, 1)
    take(-1, 1, 1, ())
    take(1, 1, 1, ())
    take(2, 1, 1, ())
    use(-1, 1, 1)
    use(1, 1, 1)
    use(2, 1, 1)
    if finish.inward:
        for t in range(2):
            finish.last(acc, side, outs, t, t + first - 2 * t * first)
    else:
        outs[0][plane] = half(acc[1])
        back.wait()
    for copy in sends:
        copy.wait_send()


class Projection:
    inward = True

    def start(side):
        side[...] = jnp.zeros_like(side)

    def each(extra, side, t, chunk, block):
        rate = extra[0][chunk]
        lanes = side.shape[2]
        wide = block.astype(jnp.float32)
        total = wide[:, :lanes] * rate[:, :lanes]
        for at in range(lanes, block.shape[1], lanes):
            total += wide[:, at:at + lanes] * rate[:, at:at + lanes]
        side[t] += total

    def last(acc, side, outs, t, row):
        width = acc.shape[2] // 3
        q, k, v = (acc[t, :, i * width:(i + 1) * width] for i in range(3))
        rate = jnp.sum(side[t], axis=1, keepdims=True)
        step = jnp.maximum(rate, 0.0) + jnp.log1p(jnp.exp(-jnp.abs(rate)))
        outs[0][row] = half(q * lax.rsqrt(jnp.sum(q * q, axis=1, keepdims=True) + 1e-06))
        outs[1][row] = half(k * lax.rsqrt(jnp.sum(k * k, axis=1, keepdims=True) + 1e-06))
        outs[2][row] = half(v)
        outs[3][row] = half(step * v)


class Mixing:
    inward = False

    def start(side):
        pass

    def each(extra, side, t, chunk, block):
        pass


def gather_matmul(x, w, extra, finish, n_out, limit, collective_id):
    pair, group, local = x.shape
    ways = lax.axis_size("head")
    wide = w.shape[2]
    vmem = pl.BlockSpec(memory_space=pltpu.VMEM)
    dma = pltpu.SemaphoreType.DMA
    out = jax.ShapeDtypeStruct((pair, group, 256), jnp.bfloat16)
    return pl.pallas_call(
        functools.partial(gather_kernel, finish, len(extra), n_out),
        out_shape=[out] * n_out,
        in_specs=[vmem, pl.BlockSpec(memory_space=pl.ANY)] + [vmem] * len(extra),
        out_specs=[vmem] * n_out,
        scratch_shapes=[
            pltpu.VMEM((ways, 2, group, local), jnp.bfloat16),
            pltpu.VMEM(w.shape, jnp.bfloat16),
            pltpu.VMEM((2, group, wide), jnp.float32),
            pltpu.VMEM((2, group, 128), jnp.float32),
            pltpu.VMEM((group, 256), jnp.bfloat16),
            dma, dma((40,)), dma((ways, 2)), dma((2,)),
        ],
        compiler_params=pltpu.CompilerParams(
            collective_id=collective_id, has_side_effects=True, vmem_limit_bytes=limit << 20
        ),
        cost_estimate=pl.CostEstimate(
            flops=2 * pair * group * ways * local * wide, bytes_accessed=10**7, transcendentals=0
        ),
    )(x, w, *extra)


def body(x, w_in, w_rate, scale, gain, a0, b0, w_out):
    ways = lax.axis_size("head")
    local = x.shape[2]
    w_in = w_in.reshape(ways, local, w_in.shape[2])
    rate = w_rate.astype(jnp.float32).reshape(ways, 1, local)
    q, k, v, g = gather_matmul(x, w_in, (rate,), Projection, 4, 50, 2)
    head_out, mixing = column(scale, gain, q, k, v, g, a0[0], b0[0], w_out[0], 1)
    (out,) = gather_matmul(head_out, mixing, (), Mixing, 1, 32, 3)
    return out


def solution(mesh):
    in_specs = (
        P(None, "seq", "head"),
        P(None, "head", None),
        P(None, "head"),
        P("head"),
        P("head", None),
        P("head", None, None),
        P("head", None, None),
        P("head", None, None),
    )
    out_specs = P(None, "seq", "head")
    return jax.shard_map(body, mesh=mesh, in_specs=in_specs, out_specs=out_specs, check_vma=False)
```

time: 248 us -> 166 us (0.67); the launches traced: 244 us -> 166 us
  Pallas kernels: 219 us -> 163 us
  local copies, waits for them, and re-layouts: 19.7 us -> 1.84 us
  starting transfers between devices: 4.16 us -> 0 us
    pallas_call x3, Pallas kernels: 219 us -> 163 us  [the longest x2 89.7 us: gather_matmul(): pl.pallas_call(functools.partial(gather_kernel, finish, len(extra), n_out...]
    unnamed x33 -> x9, local copies, waits for them, and re-layouts: 17.3 us -> 1.84 us
    all_to_all x1 -> x0, starting transfers between devices: 4.16 us -> none  [body(): lax.all_to_all(pieces, 'head', split_axis=0, concat_axis=0, tiled=True)]
  transfers between devices with their start and end apart: 1 -> 0, of which waited for: 0 -> 0; matrix products, arithmetic and copies ran while one was open for 1% -> 0% of each run, Pallas kernels for 49% -> 0%
where the time goes in v3:
time: 166 us
  Pallas kernels  163 us (98%)
  local copies, waits for them, and re-layouts  1.84 us (1%)
    pallas_call x2, Pallas kernels, gather_matmul(): pl.pallas_call(functools.partial(gather_kernel, finish, len(extra), n_out...  89.7 us
    pallas_call x1, Pallas kernels, column(): pl.pallas_call(functools.partial(column_kernel, FAR_OWNER, LATE_WINDOWS),...  73 us

profile of v3, /device:TPU:16, one launch (start us, length us, event | category | flops | bytes accessed | tf_op | source)
XLA Modules:
  0.0 166.0 jit_solution(8382746086762309915)
XLA Ops:
  0.7 0.7 convert.1.refs_2_
  1.4 0.0 copy-start
  1.4 1.0 copy-done
  2.4 0.0 copy-start.1
  2.4 0.0 copy-start.2
  2.4 0.0 copy-start.3
  2.4 46.8 %shard_map.82 = (bf16[2,512,256]{2,1,0:T(8,128)(2,1)S(1)}, bf16[2,512,256]{2,1,0:T(8,128)(2,1)S(1)}, bf16[2,512,256]{2,1,0:T(8,128)(2,1)S(1)}, bf16[2,512,256]{2,1,0:T(8,128)(2,1)S(1)}) custom-call(bf16[2,512,256]{2,1,0:T(8,128)(2,1)S(1)} %copy-done, bf16[16,256,768]{2,1,0:T(8,128)(2,1)} %bitcast.9, f32[16,1,256]{2,1,0:T(1,128)S(1)} %convert.1.refs_2_), custom_call_target="tpu_custom_call" | custom-call | flops 6442450944 | bytes 10000000 | tf_op jit(solution)/shard_map/pallas_call | solution.py:532
  49.3 0.0 copy-done.1
  49.3 0.0 copy-done.2
  49.3 0.0 copy-done.3
  49.3 73.0 %shard_map.83 = (bf16[2,512,256]{2,1,0:T(8,128)(2,1)S(1)}, bf16[16,256,256]{2,1,0:T(8,128)(2,1)S(1)}) custom-call(f32[1]{0:T(128)S(6)} %copy.10.scale_ref, f32[1,256]{1,0:T(1,128)S(1)} %copy-done.3, bf16[2,512,256]{2,1,0:T(8,128)(2,1)S(1)} %get-tuple-element.11.q_ref, bf16[2,512,256]{2,1,0:T(8,128)(2,1)S(1)} %get-tuple-element.12.k_ref, ...), custom_call_target="tpu_custom_call" | custom-call | flops 10000000000 | bytes 10000000 | tf_op jit(solution)/shard_map/pallas_call | solution.py:319
  122.3 42.9 %shard_map.84 = bf16[2,512,256]{2,1,0:T(8,128)(2,1)S(1)} custom-call(bf16[2,512,256]{2,1,0:T(8,128)(2,1)S(1)} %get-tuple-element.15.refs_0_, bf16[16,256,256]{2,1,0:T(8,128)(2,1)S(1)} %get-tuple-element.16.refs_1_), custom_call_target="tpu_custom_call" | custom-call | flops 2147483648 | bytes 10000000 | tf_op jit(solution)/shard_map/pallas_call | solution.py:532
  165.2 0.8 copy.11
Async XLA Ops:
  1.4 1.0 copy-start
  2.4 46.8 %copy-start.1 = (f32[1,256,512]{2,1,0:T(8,128)S(1)}, f32[1,256,512]{2,1,0:T(8,128)}, u32[]{:S(2)}) copy-start(f32[1,256,512]{2,1,0:T(8,128)} %param.13) | copy-start | bytes 1572868
  2.4 46.8 %copy-start.2 = (f32[1,512,256]{2,1,0:T(8,128)S(1)}, f32[1,512,256]{2,1,0:T(8,128)}, u32[]{:S(2)}) copy-start(f32[1,512,256]{2,1,0:T(8,128)} %param.14) | copy-start | bytes 1572868
  2.4 46.8 %copy-start.3 = (f32[1,256]{1,0:T(1,128)S(1)}, f32[1,256]{1,0:T(1,128)}, u32[]{:S(2)}) copy-start(f32[1,256]{1,0:T(1,128)} %gain_ref.1) | copy-start | bytes 3076

commit v4 on v3

v4 whole, which is shorter than its diff:
```python
import functools
import jax
import jax.numpy as jnp
from jax import lax
from jax.experimental import pallas as pl
from jax.experimental.pallas import tpu as pltpu
from jax.sharding import PartitionSpec as P

WIN = 2048
NS_STEPS = 3
UPDATE_RATE = 0.3
LOG2E = 1.4426950408889634
MESH = pl.DeviceIdType.MESH
NT = (((1,), (1,)), ((), ()))
TN = (((0,), (0,)), ((), ()))
NN = (((1,), (0,)), ((), ()))


def mm(a, b, dims=NN):
    return lax.dot_general(a, b, dims, preferred_element_type=jnp.float32)


def half(a):
    return a.astype(jnp.bfloat16)


def sigmoid(a):
    return 0.5 * jnp.tanh(0.5 * a) + 0.5


def unit_scaled(update):
    return update * lax.rsqrt(jnp.sum(update * update) + 1e-06)


def chain_step(state_a, state_b, k, g):
    hidden = mm(k, half(state_a[...]))
    back = mm(g, half(state_b[...]))
    gate = sigmoid(hidden)
    act = half(hidden * gate)
    slopes = half(back * gate * (1.0 + hidden * (1.0 - gate)))
    xa = unit_scaled(mm(k, slopes, TN))
    xb = unit_scaled(mm(g, act, TN))
    for _ in range(NS_STEPS):
        ha, hb = half(xa), half(xb)
        gram_a = half(mm(ha, ha, NT))
        gram_b = half(mm(hb, hb, NT))
        xa = 1.5 * xa - 0.5 * mm(gram_a, ha)
        xb = 1.5 * xb - 0.5 * mm(gram_b, hb)
    state_a[...] += UPDATE_RATE * xa
    state_b[...] += UPDATE_RATE * xb


def ring_of(p):
    return p // 2, p % 2


def front_kernel(
    scale_ref, gain_ref, x_ref, w_hbm, rate_ref, a0_ref, b0_ref, w_ref, out_ref, mix_ref,
    held, weights, pacc, side, q_ref, k_ref, v_ref, t_ref, kwin, vwin, twin_ref,
    state_a, state_b, top, total, acc,
    w_sem, send_sem, recv_sem, out_sem, win_sem, mix_send, mix_recv, mix_own,
):
    p = lax.axis_index("seq")
    h = lax.axis_index("head")
    y, plane = ring_of(p)
    ways = lax.axis_size("head")
    ring = lax.axis_size("seq") // 2
    pair, group, width = q_ref.shape
    early, late = plane, 1 - plane

    def place(row):
        return ((row + ring) % ring) * 2 + plane

    load = pltpu.make_async_copy(w_hbm, weights, w_sem)
    load.start()
    barrier = pltpu.get_barrier_semaphore()
    pl.semaphore_signal(barrier, inc=1, device_id=(2 * y + 1 - plane, h), device_id_type=MESH)
    for d in range(1, ways):
        pl.semaphore_signal(barrier, inc=1, device_id=(p, (h + d) % ways), device_id_type=MESH)
    for d in range(1, ring):
        pl.semaphore_signal(barrier, inc=1, device_id=(place(y + d), h), device_id_type=MESH)
    pl.semaphore_wait(barrier, ways + ring - 1)

    pieces = ((k_ref, kwin), (v_ref, vwin), (t_ref, twin_ref))
    to_next, to_back, relayed = 0, 1, 2

    def outgoing(site, j, which, src, target, slot):
        return pltpu.make_async_remote_copy(
            src_ref=src, dst_ref=pieces[which][1].at[slot, j],
            send_sem=out_sem.at[site, j, which], recv_sem=win_sem.at[slot, j, which],
            device_id=(place(target), h), device_id_type=MESH,
        )

    def next_copy(j, which):
        return outgoing(to_next, j, which, pieces[which][0].at[j], y + 1, 0)

    def back_copy(j, which):
        return outgoing(to_back, j, which, pieces[which][0].at[j], y - 1, 2)

    def goes_next():
        return y < ring - 1

    def goes_back(j):
        return (y == 0) | ((y == 1) & (j == 0))

    def project(t, row):
        q, k, v = (pacc[t, :, i * width:(i + 1) * width] for i in range(3))
        q_ref[row] = half(q * lax.rsqrt(jnp.sum(q * q, axis=1, keepdims=True) + 1e-06))
        k_ref[row] = half(k * lax.rsqrt(jnp.sum(k * k, axis=1, keepdims=True) + 1e-06))
        v_ref[row] = half(v)
        rate = jnp.sum(side[t], axis=1, keepdims=True)
        step = jnp.maximum(rate, 0.0) + jnp.log1p(jnp.exp(-jnp.abs(rate)))
        t_ref[row] = jnp.broadcast_to(step, (group, 128)).T[:8]
        for which in range(3):
            pl.when(goes_back(row))(back_copy(row, which).start)
            pl.when(goes_next())(next_copy(row, which).start)

    def each(t, chunk, block):
        rate = rate_ref[chunk]
        wide = block.astype(jnp.float32)
        part = wide[:, :128] * rate[:, :128]
        for at in range(128, width, 128):
            part += wide[:, at:at + 128] * rate[:, at:at + 128]
        side[t] += part

    side[...] = jnp.zeros_like(side)
    gather(
        p, h, plane, early, True, x_ref, held, weights, pacc, load, send_sem, recv_sem,
        each, lambda: project(0, early),
    )
    project(1, late)

    def mixing(d):
        other = (h + d) % ways
        return pltpu.make_async_remote_copy(
            src_ref=w_ref.at[:, pl.ds(pl.multiple_of(other * width, width), width)],
            dst_ref=mix_ref.at[h],
            send_sem=mix_send.at[d], recv_sem=mix_recv.at[d],
            device_id=(p, other), device_id_type=MESH,
        )

    mine = pltpu.make_async_copy(
        w_ref.at[:, pl.ds(pl.multiple_of(h * width, width), width)], mix_ref.at[h], mix_own
    )
    mine.start()
    for d in range(1, ways):
        mixing(d).start()

    state_a[...] = a0_ref[...]
    state_b[...] = b0_ref[...].T

    sharp = scale_ref[0] * LOG2E
    tile = group // 2

    def score(j, r, keys, edge):
        rows = pl.ds(pl.multiple_of(r * tile, tile), tile)
        sc = mm(q_ref[j, rows], keys, NT) * sharp
        if edge:
            row = lax.broadcasted_iota(jnp.int32, sc.shape, 0) + r * tile
            col = lax.broadcasted_iota(jnp.int32, sc.shape, 1)
            sc = jnp.where((col <= row) if edge == 1 else (col >= row), sc, -1e30)
        return rows, sc

    def first(i, carry):
        j, r = i // 2, i % 2
        rows, sc = score(j, r, k_ref[j], 1)
        high = jnp.max(sc, axis=1, keepdims=True)
        w = jnp.exp2(sc - high)
        top[j, rows] = high
        total[j, rows] = jnp.sum(w, axis=1, keepdims=True)
        acc[j, rows] = mm(half(w), v_ref[j])
        return carry

    def fold(j, r, keys, values, edge):
        rows, sc = score(j, r, keys, edge)
        old = top[j, rows]
        high = jnp.maximum(old, jnp.max(sc, axis=1, keepdims=True))
        w = jnp.exp2(sc - high)
        shrink = jnp.exp2(old - high)
        top[j, rows] = high
        total[j, rows] = total[j, rows] * shrink + jnp.sum(w, axis=1, keepdims=True)
        acc[j, rows] = acc[j, rows] * shrink + mm(half(w), values)

    def arrive(slot, j):
        for which in range(3):
            pltpu.make_async_remote_copy(
                src_ref=pieces[which][1].at[slot, j], dst_ref=pieces[which][1].at[slot, j],
                send_sem=out_sem.at[0, 0, which], recv_sem=win_sem.at[slot, j, which],
                device_id=(place(y + 1), h), device_id_type=MESH,
            ).wait_recv()

    def relay(slot, j, target):
        for which in range(3):
            outgoing(relayed, j, which, pieces[which][1].at[slot, j], target, 1).start()

    def learn(k, v, t):
        steps = t.T[:, :1]
        chain_step(state_a, state_b, k, half(v.astype(jnp.float32) * steps))

    def learn_pair(slot):
        def turn(j, carry):
            learn(kwin[slot, j], vwin[slot, j], twin_ref[slot, j])
            return carry

        lax.fori_loop(0, pair, turn, 0)

    def near(b):
        def turn(i, carry):
            fold(i // 2, i % 2, kwin[0, b], vwin[0, b], 0)
            return carry

        lax.fori_loop(0, 2 * pair, turn, 0)

    lax.fori_loop(0, 2 * pair, first, 0)

    def own(r, carry):
        fold(1, r, k_ref[0], v_ref[0], 0)
        return carry

    lax.fori_loop(0, 2, own, 0)

    @pl.when(y == 0)
    def _():
        arrive(2, 0)
        relay(2, 0, y - 1)

    @pl.when(y == 2)
    def _():
        arrive(0, 1)
        relay(0, 1, y + 1)
        arrive(0, 0)

    @pl.when(y == 3)
    def _():
        arrive(2, early)
        relay(2, early, y - 1)

    @pl.when((y == 1) | (y == 3))
    def _():
        arrive(0, early)

    pl.when(y >= 1)(lambda: near(early))

    @pl.when(y == 3)
    def _():
        arrive(2, late)
        relay(2, late, y - 1)
        learn_pair(2)

    @pl.when(y >= 2)
    def _():
        arrive(1, 0)
        arrive(1, 1)

        def edge(i, carry):
            j = i // 2
            fold(j, i % 2, kwin[1, j], vwin[1, j], 2)
            return carry

        lax.fori_loop(0, 4, edge, 0)

        def inner(r, carry):
            fold(0, r, kwin[1, 1], vwin[1, 1], 0)
            return carry

        lax.fori_loop(0, 2, inner, 0)
        learn_pair(1)

    @pl.when((y == 1) | (y == 3))
    def _():
        arrive(0, late)

    @pl.when(y >= 1)
    def _():
        near(late)
        learn_pair(0)

    def answer(j, carry):
        learn(k_ref[j], v_ref[j], t_ref[j])
        hidden = mm(q_ref[j], half(state_a[...]))
        act = half(hidden * sigmoid(hidden))
        fast = mm(act, half(state_b[...]), NT)
        fast = fast * lax.rsqrt(jnp.mean(fast * fast, axis=1, keepdims=True) + 1e-05)
        out_ref[j] = half(acc[j] / total[j] + fast * gain_ref[...])
        return carry

    lax.fori_loop(0, pair, answer, 0)

    for j in range(pair):
        for which in range(3):
            pl.when(goes_next())(next_copy(j, which).wait_send)
            pl.when(goes_back(j))(back_copy(j, which).wait_send)
            moved = (y == 3) | ((y == 0) & (j == 0)) | ((y == 2) & (j == 1))
            pl.when(moved)(
                outgoing(relayed, j, which, pieces[which][1].at[2, j], y - 1, 1).wait_send
            )
    mine.wait()
    for d in range(1, ways):
        mixing(d).wait_send()
        source = (h - d + ways) % ways
        pltpu.make_async_remote_copy(
            src_ref=mix_ref.at[source], dst_ref=mix_ref.at[source],
            send_sem=mix_send.at[d], recv_sem=mix_recv.at[d],
            device_id=(p, (h + d) % ways), device_id_type=MESH,
        ).wait_recv()


def front(scale, gain, x, w_in, rate, a0, b0, w_out, collective_id):
    pair, group, width = x.shape
    hid = a0.shape[1]
    ways = lax.axis_size("head")
    ring = lax.axis_size("seq") // 2
    vmem = pl.BlockSpec(memory_space=pltpu.VMEM)
    hbm = pl.BlockSpec(memory_space=pl.ANY)
    dma = pltpu.SemaphoreType.DMA
    bf16, f32 = jnp.bfloat16, jnp.float32
    block = pltpu.VMEM((pair, group, width), bf16)
    window = pltpu.VMEM((ring - 1, pair, group, width), bf16)
    return pl.pallas_call(
        front_kernel,
        out_shape=[
            jax.ShapeDtypeStruct(x.shape, bf16),
            jax.ShapeDtypeStruct((ways, width, width), bf16),
        ],
        in_specs=[pl.BlockSpec(memory_space=pltpu.SMEM), vmem, vmem, hbm, vmem, vmem, vmem, hbm],
        out_specs=[vmem, vmem],
        scratch_shapes=[
            pltpu.VMEM((ways, pair, group, width), bf16),
            pltpu.VMEM(w_in.shape, bf16),
            pltpu.VMEM((pair, group, w_in.shape[2]), f32),
            pltpu.VMEM((pair, group, 128), f32),
            block, block, block,
            pltpu.VMEM((pair, 8, group), f32),
            window, window,
            pltpu.VMEM((ring - 1, pair, 8, group), f32),
            pltpu.VMEM((width, hid), f32),
            pltpu.VMEM((width, hid), f32),
            pltpu.VMEM((pair, group, 1), f32),
            pltpu.VMEM((pair, group, 1), f32),
            pltpu.VMEM((pair, group, width), f32),
            dma, dma((40,)), dma((ways, 2)),
            dma((3, pair, 3)), dma((ring - 1, pair, 3)),
            dma((ways,)), dma((ways,)), dma,
        ],
        compiler_params=pltpu.CompilerParams(
            collective_id=collective_id, has_side_effects=True, vmem_limit_bytes=50 << 20
        ),
        cost_estimate=pl.CostEstimate(
            flops=2 * 10**10, bytes_accessed=10**7, transcendentals=10**6
        ),
    )(scale, gain, x, w_in, rate, a0, b0, w_out)


def gather(
    p, me, plane, first, inward, x_ref, held, weights, acc, load, send_sem, recv_sem, each, middle
):
    partner = 2 * (p // 2) + 1 - plane
    x, z, core = me // 4, (me // 2) % 2, me % 2

    def at(dx, dz, dc):
        return ((x + dx + 4) % 4) * 4 + ((z + dz) % 2) * 2 + (core + dc) % 2

    plus, minus, across, twin = at(1, 0, 0), at(-1, 0, 0), at(0, 1, 0), at(0, 0, 1)
    sends = []

    def send(chunk, t, target, source=None):
        copy = pltpu.make_async_remote_copy(
            src_ref=held.at[chunk, t] if source is None else source,
            dst_ref=held.at[chunk, t],
            send_sem=send_sem.at[len(sends)],
            recv_sem=recv_sem.at[chunk, t],
            device_id=target, device_id_type=MESH,
        )
        copy.start()
        sends.append(copy)

    def arrived(chunk, t):
        pltpu.make_async_remote_copy(
            src_ref=held.at[chunk, t], dst_ref=held.at[chunk, t],
            send_sem=send_sem.at[0], recv_sem=recv_sem.at[chunk, t],
            device_id=(p, twin), device_id_type=MESH,
        ).wait_recv()

    if inward:
        send(me, 1, (partner, me), x_ref.at[1 - first])
    for other in (plus, minus, across, twin):
        send(me, 0, (p, other), x_ref.at[first])
    if not inward:
        for other in (minus, plus, across, twin):
            send(me, 1, (p, other), x_ref.at[1 - first])
        held[me, 1] = x_ref[1 - first]
    held[me, 0] = x_ref[first]

    acc[...] = jnp.zeros_like(acc)
    load.wait()

    def take(dx, dz, t, targets):
        chunk = at(dx, dz, 0)
        arrived(chunk, t)
        for target in targets:
            send(chunk, t, (p, target))
        send(chunk, t, (p, twin))

    def use(dx, dz, t):
        here, there = at(dx, dz, 0), at(dx, dz, 1)
        arrived(there, t)

        def step(i, carry):
            chunk = here + i * (there - here)
            block = held[chunk, t]
            acc[t] += mm(block, weights[chunk])
            each(t, chunk, block)
            return carry

        lax.fori_loop(0, 2, step, 0)

    take(-1, 0, 0, (plus,))
    take(0, 1, 0, (plus, minus))
    take(1, 0, 0, ())
    if inward:
        arrived(me, 1)
        for other in (minus, plus, across, twin):
            send(me, 1, (p, other))
    use(0, 0, 0)
    use(-1, 0, 0)
    use(0, 1, 0)
    use(1, 0, 0)
    take(1, 0, 1, (minus,))
    take(0, 1, 1, (minus, plus))
    take(-1, 0, 1, ())
    take(2, 0, 0, (across,))
    use(0, 0, 1)
    use(2, 0, 0)
    take(-1, 1, 0, ())
    take(1, 1, 0, ())
    use(1, 0, 1)
    use(0, 1, 1)
    use(-1, 0, 1)
    take(2, 0, 1, (across,))
    take(2, 1, 0, ())
    use(-1, 1, 0)
    use(1, 1, 0)
    use(2, 1, 0)
    middle()
    use(2, 0, 1)
    take(-1, 1, 1, ())
    take(1, 1, 1, ())
    take(2, 1, 1, ())
    use(-1, 1, 1)
    use(1, 1, 1)
    use(2, 1, 1)
    for copy in sends:
        copy.wait_send()


def mixing_kernel(
    x_ref, w_hbm, out_ref, held, weights, acc, stage, w_sem, send_sem, recv_sem, swap_sem
):
    p = lax.axis_index("seq")
    me = lax.axis_index("head")
    y, plane = ring_of(p)
    partner = 2 * y + 1 - plane

    load = pltpu.make_async_copy(w_hbm, weights, w_sem)
    load.start()
    barrier = pltpu.get_barrier_semaphore()
    pl.semaphore_signal(barrier, inc=1, device_id=(partner, me), device_id_type=MESH)
    x, z, core = me // 4, (me // 2) % 2, me % 2
    for other in (
        ((x + 1) % 4) * 4 + z * 2 + core, ((x + 3) % 4) * 4 + z * 2 + core,
        x * 4 + (1 - z) * 2 + core, x * 4 + z * 2 + 1 - core,
    ):
        pl.semaphore_signal(barrier, inc=1, device_id=(p, other), device_id_type=MESH)
    pl.semaphore_wait(barrier, 5)

    back = pltpu.make_async_remote_copy(
        src_ref=stage, dst_ref=out_ref.at[plane],
        send_sem=swap_sem.at[0], recv_sem=swap_sem.at[1],
        device_id=(partner, me), device_id_type=MESH,
    )

    def middle():
        stage[...] = half(acc[0])
        back.start()

    gather(
        p, me, plane, 1 - plane, False, x_ref, held, weights, acc, load, send_sem, recv_sem,
        lambda t, chunk, block: None, middle,
    )
    out_ref[plane] = half(acc[1])
    back.wait()


def mix(x, w, collective_id):
    pair, group, local = x.shape
    ways, _, wide = w.shape
    vmem = pl.BlockSpec(memory_space=pltpu.VMEM)
    dma = pltpu.SemaphoreType.DMA
    return pl.pallas_call(
        mixing_kernel,
        out_shape=jax.ShapeDtypeStruct((pair, group, wide), jnp.bfloat16),
        in_specs=[vmem, pl.BlockSpec(memory_space=pl.ANY)],
        out_specs=vmem,
        scratch_shapes=[
            pltpu.VMEM((ways, pair, group, local), jnp.bfloat16),
            pltpu.VMEM(w.shape, jnp.bfloat16),
            pltpu.VMEM((pair, group, wide), jnp.float32),
            pltpu.VMEM((group, wide), jnp.bfloat16),
            dma, dma((40,)), dma((ways, 2)), dma((2,)),
        ],
        compiler_params=pltpu.CompilerParams(
            collective_id=collective_id, has_side_effects=True, vmem_limit_bytes=32 << 20
        ),
        cost_estimate=pl.CostEstimate(
            flops=2 * pair * group * ways * local * wide, bytes_accessed=10**7, transcendentals=0
        ),
    )(x, w)


def body(x, w_in, w_rate, scale, gain, a0, b0, w_out):
    ways = lax.axis_size("head")
    local = x.shape[2]
    w_in = w_in.reshape(ways, local, w_in.shape[2])
    rate = w_rate.astype(jnp.float32).reshape(ways, 1, local)
    head_out, mixing = front(scale, gain, x, w_in, rate, a0[0], b0[0], w_out[0], 1)
    return mix(head_out, mixing, 2)


def solution(mesh):
    in_specs = (
        P(None, "seq", "head"),
        P(None, "head", None),
        P(None, "head"),
        P("head"),
        P("head", None),
        P("head", None, None),
        P("head", None, None),
        P("head", None, None),
    )
    out_specs = P(None, "seq", "head")
    return jax.shard_map(body, mesh=mesh, in_specs=in_specs, out_specs=out_specs, check_vma=False)
```

time: 166 us -> 157 us (0.946)
  Pallas kernels: 163 us -> 149 us
  local copies, waits for them, and re-layouts: 1.84 us -> 6.18 us
    pallas_call x3 -> x2, Pallas kernels: 163 us -> 149 us  [the longest x1 105 us: front(): pl.pallas_call(front_kernel, out_shape=[jax.ShapeDtypeStruct(x.shape, bf1...]
    unnamed x9 -> x11, local copies, waits for them, and re-layouts: 1.84 us -> 6.18 us
where the time goes in v4:
time: 157 us; the launch traced here: 156 us
  Pallas kernels  149 us (95%)
  local copies, waits for them, and re-layouts  6.18 us (4%)
    pallas_call x1, Pallas kernels, front(): pl.pallas_call(front_kernel, out_shape=[jax.ShapeDtypeStruct(x.shape, bf1...  105 us
    pallas_call x1, Pallas kernels, mix(): pl.pallas_call(mixing_kernel, out_shape=jax.ShapeDtypeStruct((pair, group...  43.5 us
    unnamed x11, local copies, waits for them, and re-layouts  6.18 us

profile of v4, /device:TPU:16, one launch (start us, length us, event | category | flops | bytes accessed | tf_op | source)
XLA Modules:
  0.0 156.4 jit_solution(12392944647028094521)
XLA Ops:
  0.7 0.7 convert.1.rate_ref
  1.4 0.0 copy-start
  1.4 1.0 copy-done
  2.4 0.0 copy-start.1
  2.4 1.0 copy-done.1
  3.5 0.0 copy-start.2
  3.5 1.0 copy-done.2
  4.5 0.0 copy-start.3
  4.5 0.7 copy-done.3
  5.2 105.3 %shard_map.82 = (bf16[2,512,256]{2,1,0:T(8,128)(2,1)S(1)}, bf16[16,256,256]{2,1,0:T(8,128)(2,1)}) custom-call(f32[1]{0:T(128)S(6)} %copy.10.scale_ref, f32[1,256]{1,0:T(1,128)S(1)} %copy-done.3, bf16[2,512,256]{2,1,0:T(8,128)(2,1)S(1)} %copy-done, bf16[16,256,768]{2,1,0:T(8,128)(2,1)} %bitcast.9, f32[16,1,256]{2,1,0:T(1,128)S(1)} %convert.1.rate_ref, ...), custom_call_target="tpu_custom_call" | custom-call | flops 20000000000 | bytes 10000000 | tf_op jit(solution)/shard_map/pallas_call | solution.py:319
  110.5 0.0 copy-start.4
  110.5 1.6 %copy-done.4 = bf16[16,256,256]{2,1,0:T(8,128)(2,1)S(1)} copy-done((bf16[16,256,256]{2,1,0:T(8,128)(2,1)S(1)}, bf16[16,256,256]{2,1,0:T(8,128)(2,1)}, u32[]{:S(2)}) %copy-start.4) | copy-done | bytes 2097176
  112.1 43.5 %shard_map.83 = bf16[2,512,256]{2,1,0:T(8,128)(2,1)S(1)} custom-call(bf16[2,512,256]{2,1,0:T(8,128)(2,1)S(1)} %get-tuple-element.7.x_ref, bf16[16,256,256]{2,1,0:T(8,128)(2,1)S(1)} %copy-done.4), custom_call_target="tpu_custom_call" | custom-call | flops 2147483648 | bytes 10000000 | tf_op jit(solution)/shard_map/pallas_call | solution.py:499
  155.6 0.8 copy.11
Async XLA Ops:
  1.4 1.0 copy-start
  2.4 1.0 copy-start.1
  3.5 1.0 copy-start.2
  4.5 0.7 copy-start.3
  110.5 1.6 %copy-start.4 = (bf16[16,256,256]{2,1,0:T(8,128)(2,1)S(1)}, bf16[16,256,256]{2,1,0:T(8,128)(2,1)}, u32[]{:S(2)}) copy-start(bf16[16,256,256]{2,1,0:T(8,128)(2,1)} %get-tuple-element.8.w_hbm) | copy-start | bytes 6291460

commit v5 on v4

--- a/solution.py
+++ b/solution.py
@@ -9,6 +9,8 @@
 WIN = 2048
 NS_STEPS = 3
 UPDATE_RATE = 0.3
+SPLIT_IN = 2
+SPLIT_OUT = 1
 LOG2E = 1.4426950408889634
 MESH = pl.DeviceIdType.MESH
 NT = (((1,), (1,)), ((), ()))
@@ -54,11 +56,13 @@
     return p // 2, p % 2
 
 
-def front_kernel(
-    scale_ref, gain_ref, x_ref, w_hbm, rate_ref, a0_ref, b0_ref, w_ref, out_ref, mix_ref,
+def layer_kernel(
+    scale_ref, gain_ref, x_ref, w_hbm, rate_ref, a0_ref, b0_ref, w_ref, out_ref,
     held, weights, pacc, side, q_ref, k_ref, v_ref, t_ref, kwin, vwin, twin_ref,
     state_a, state_b, top, total, acc,
+    mix_ref, heads, held_heads, mixed, stage,
     w_sem, send_sem, recv_sem, out_sem, win_sem, mix_send, mix_recv, mix_own,
+    send_heads, recv_heads, swap_sem,
 ):
     p = lax.axis_index("seq")
     h = lax.axis_index("head")
@@ -125,7 +129,7 @@
 
     side[...] = jnp.zeros_like(side)
     gather(
-        p, h, plane, early, True, x_ref, held, weights, pacc, load, send_sem, recv_sem,
+        p, h, plane, early, True, SPLIT_IN, x_ref, held, weights, pacc, load.wait, send_sem, recv_sem,
         each, lambda: project(0, early),
     )
     project(1, late)
@@ -247,33 +251,27 @@
         relay(2, late, y - 1)
         learn_pair(2)
 
+    @pl.when((y == 1) | (y == 3))
+    def _():
+        arrive(0, late)
+
+    pl.when(y >= 1)(lambda: near(late))
+
     @pl.when(y >= 2)
     def _():
         arrive(1, 0)
         arrive(1, 1)
 
-        def edge(i, carry):
-            j = i // 2
-            fold(j, i % 2, kwin[1, j], vwin[1, j], 2)
+        def turn(j, carry):
+            learn(kwin[1, j], vwin[1, j], twin_ref[1, j])
+            for r in range(2):
+                fold(j, r, kwin[1, j], vwin[1, j], 2)
+            fold(0, j, kwin[1, 1], vwin[1, 1], 0)
             return carry
 
-        lax.fori_loop(0, 4, edge, 0)
-
-        def inner(r, carry):
-            fold(0, r, kwin[1, 1], vwin[1, 1], 0)
-            return carry
-
-        lax.fori_loop(0, 2, inner, 0)
-        learn_pair(1)
-
-    @pl.when((y == 1) | (y == 3))
-    def _():
-        arrive(0, late)
-
-    @pl.when(y >= 1)
-    def _():
-        near(late)
-        learn_pair(0)
+        lax.fori_loop(0, pair, turn, 0)
+
+    pl.when(y >= 1)(lambda: learn_pair(0))
 
     def answer(j, carry):
         learn(k_ref[j], v_ref[j], t_ref[j])
@@ -281,11 +279,39 @@
         act = half(hidden * sigmoid(hidden))
         fast = mm(act, half(state_b[...]), NT)
         fast = fast * lax.rsqrt(jnp.mean(fast * fast, axis=1, keepdims=True) + 1e-05)
-        out_ref[j] = half(acc[j] / total[j] + fast * gain_ref[...])
+        heads[j] = half(acc[j] / total[j] + fast * gain_ref[...])
         return carry
 
-    lax.fori_loop(0, pair, answer, 0)
-
+    for j in range(pair):
+        answer(j, 0)
+
+    def ready():
+        mine.wait()
+        for d in range(1, ways):
+            mixing(d).wait_send()
+            source = (h - d + ways) % ways
+            pltpu.make_async_remote_copy(
+                src_ref=mix_ref.at[source], dst_ref=mix_ref.at[source],
+                send_sem=mix_send.at[d], recv_sem=mix_recv.at[d],
+                device_id=(p, (h + d) % ways), device_id_type=MESH,
+            ).wait_recv()
+
+    back = pltpu.make_async_remote_copy(
+        src_ref=stage, dst_ref=out_ref.at[plane],
+        send_sem=swap_sem.at[0], recv_sem=swap_sem.at[1],
+        device_id=(2 * y + 1 - plane, h), device_id_type=MESH,
+    )
+
+    def send_back():
+        stage[...] = half(mixed[0])
+        back.start()
+
+    gather(
+        p, h, plane, 1 - plane, False, SPLIT_OUT, heads, held_heads, mix_ref, mixed, ready,
+        send_heads, recv_heads, lambda t, chunk, block: None, send_back,
+    )
+    out_ref[plane] = half(mixed[1])
+    back.wait()
     for j in range(pair):
         for which in range(3):
             pl.when(goes_next())(next_copy(j, which).wait_send)
@@ -294,18 +320,9 @@
             pl.when(moved)(
                 outgoing(relayed, j, which, pieces[which][1].at[2, j], y - 1, 1).wait_send
             )
-    mine.wait()
-    for d in range(1, ways):
-        mixing(d).wait_send()
-        source = (h - d + ways) % ways
-        pltpu.make_async_remote_copy(
-            src_ref=mix_ref.at[source], dst_ref=mix_ref.at[source],
-            send_sem=mix_send.at[d], recv_sem=mix_recv.at[d],
-            device_id=(p, (h + d) % ways), device_id_type=MESH,
-        ).wait_recv()
-
-
-def front(scale, gain, x, w_in, rate, a0, b0, w_out, collective_id):
+
+
+def layer(scale, gain, x, w_in, rate, a0, b0, w_out, collective_id):
     pair, group, width = x.shape
     hid = a0.shape[1]
     ways = lax.axis_size("head")
@@ -317,13 +334,10 @@
     block = pltpu.VMEM((pair, group, width), bf16)
     window = pltpu.VMEM((ring - 1, pair, group, width), bf16)
     return pl.pallas_call(
-        front_kernel,
-        out_shape=[
-            jax.ShapeDtypeStruct(x.shape, bf16),
-            jax.ShapeDtypeStruct((ways, width, width), bf16),
-        ],
+        layer_kernel,
+        out_shape=jax.ShapeDtypeStruct(x.shape, bf16),
         in_specs=[pl.BlockSpec(memory_space=pltpu.SMEM), vmem, vmem, hbm, vmem, vmem, vmem, hbm],
-        out_specs=[vmem, vmem],
+        out_specs=vmem,
         scratch_shapes=[
             pltpu.VMEM((ways, pair, group, width), bf16),
             pltpu.VMEM(w_in.shape, bf16),
@@ -338,9 +352,15 @@
             pltpu.VMEM((pair, group, 1), f32),
             pltpu.VMEM((pair, group, 1), f32),
             pltpu.VMEM((pair, group, width), f32),
-            dma, dma((40,)), dma((ways, 2)),
+            pltpu.VMEM((ways, width, width), bf16),
+            block,
+            pltpu.VMEM((ways, pair, group, width), bf16),
+            pltpu.VMEM((pair, group, width), f32),
+            pltpu.VMEM((group, width), bf16),
+            dma, dma((40 * SPLIT_IN,)), dma((ways, 2, SPLIT_IN)),
             dma((3, pair, 3)), dma((ring - 1, pair, 3)),
             dma((ways,)), dma((ways,)), dma,
+            dma((40 * SPLIT_OUT,)), dma((ways, 2, SPLIT_OUT)), dma((2,)),
         ],
         compiler_params=pltpu.CompilerParams(
             collective_id=collective_id, has_side_effects=True, vmem_limit_bytes=50 << 20
@@ -352,7 +372,7 @@
 
 
 def gather(
-    p, me, plane, first, inward, x_ref, held, weights, acc, load, send_sem, recv_sem, each, middle
+    p, me, plane, first, inward, split, x_ref, held, weights, acc, ready, send_sem, recv_sem, each, middle
 ):
     partner = 2 * (p // 2) + 1 - plane
     x, z, core = me // 4, (me // 2) % 2, me % 2
@@ -363,23 +383,29 @@
     plus, minus, across, twin = at(1, 0, 0), at(-1, 0, 0), at(0, 1, 0), at(0, 0, 1)
     sends = []
 
-    def send(chunk, t, target, source=None):
-        copy = pltpu.make_async_remote_copy(
-            src_ref=held.at[chunk, t] if source is None else source,
-            dst_ref=held.at[chunk, t],
-            send_sem=send_sem.at[len(sends)],
-            recv_sem=recv_sem.at[chunk, t],
-            device_id=target, device_id_type=MESH,
-        )
-        copy.start()
-        sends.append(copy)
-
-    def arrived(chunk, t):
-        pltpu.make_async_remote_copy(
-            src_ref=held.at[chunk, t], dst_ref=held.at[chunk, t],
-            send_sem=send_sem.at[0], recv_sem=recv_sem.at[chunk, t],
-            device_id=(p, twin), device_id_type=MESH,
-        ).wait_recv()
+    cut = held.shape[2] // split
+
+    def send(chunk, t, target, source=None, parts=range(split)):
+        for u in parts:
+            rows = pl.ds(u * cut, cut)
+            copy = pltpu.make_async_remote_copy(
+                src_ref=held.at[chunk, t, rows] if source is None else source.at[rows],
+                dst_ref=held.at[chunk, t, rows],
+                send_sem=send_sem.at[len(sends)],
+                recv_sem=recv_sem.at[chunk, t, u],
+                device_id=target, device_id_type=MESH,
+            )
+            copy.start()
+            sends.append(copy)
+
+    def arrived(chunk, t, parts=range(split)):
+        for u in parts:
+            rows = pl.ds(u * cut, cut)
+            pltpu.make_async_remote_copy(
+                src_ref=held.at[chunk, t, rows], dst_ref=held.at[chunk, t, rows],
+                send_sem=send_sem.at[0], recv_sem=recv_sem.at[chunk, t, u],
+                device_id=(p, twin), device_id_type=MESH,
+            ).wait_recv()
 
     if inward:
         send(me, 1, (partner, me), x_ref.at[1 - first])
@@ -392,14 +418,15 @@
     held[me, 0] = x_ref[first]
 
     acc[...] = jnp.zeros_like(acc)
-    load.wait()
+    ready()
 
     def take(dx, dz, t, targets):
         chunk = at(dx, dz, 0)
-        arrived(chunk, t)
-        for target in targets:
-            send(chunk, t, (p, target))
-        send(chunk, t, (p, twin))
+        for u in range(split):
+            arrived(chunk, t, (u,))
+            for target in targets:
+                send(chunk, t, (p, target), None, (u,))
+            send(chunk, t, (p, twin), None, (u,))
 
     def use(dx, dz, t):
         here, there = at(dx, dz, 0), at(dx, dz, 1)
@@ -418,9 +445,10 @@
     take(0, 1, 0, (plus, minus))
     take(1, 0, 0, ())
     if inward:
-        arrived(me, 1)
-        for other in (minus, plus, across, twin):
-            send(me, 1, (p, other))
+        for u in range(split):
+            arrived(me, 1, (u,))
+            for other in (minus, plus, across, twin):
+                send(me, 1, (p, other), None, (u,))
     use(0, 0, 0)
     use(-1, 0, 0)
     use(0, 1, 0)
@@ -453,77 +481,12 @@
         copy.wait_send()
 
 
-def mixing_kernel(
-    x_ref, w_hbm, out_ref, held, weights, acc, stage, w_sem, send_sem, recv_sem, swap_sem
-):
-    p = lax.axis_index("seq")
-    me = lax.axis_index("head")
-    y, plane = ring_of(p)
-    partner = 2 * y + 1 - plane
-
-    load = pltpu.make_async_copy(w_hbm, weights, w_sem)
-    load.start()
-    barrier = pltpu.get_barrier_semaphore()
-    pl.semaphore_signal(barrier, inc=1, device_id=(partner, me), device_id_type=MESH)
-    x, z, core = me // 4, (me // 2) % 2, me % 2
-    for other in (
-        ((x + 1) % 4) * 4 + z * 2 + core, ((x + 3) % 4) * 4 + z * 2 + core,
-        x * 4 + (1 - z) * 2 + core, x * 4 + z * 2 + 1 - core,
-    ):
-        pl.semaphore_signal(barrier, inc=1, device_id=(p, other), device_id_type=MESH)
-    pl.semaphore_wait(barrier, 5)
-
-    back = pltpu.make_async_remote_copy(
-        src_ref=stage, dst_ref=out_ref.at[plane],
-        send_sem=swap_sem.at[0], recv_sem=swap_sem.at[1],
-        device_id=(partner, me), device_id_type=MESH,
-    )
-
-    def middle():
-        stage[...] = half(acc[0])
-        back.start()
-
-    gather(
-        p, me, plane, 1 - plane, False, x_ref, held, weights, acc, load, send_sem, recv_sem,
-        lambda t, chunk, block: None, middle,
-    )
-    out_ref[plane] = half(acc[1])
-    back.wait()
-
-
-def mix(x, w, collective_id):
-    pair, group, local = x.shape
-    ways, _, wide = w.shape
-    vmem = pl.BlockSpec(memory_space=pltpu.VMEM)
-    dma = pltpu.SemaphoreType.DMA
-    return pl.pallas_call(
-        mixing_kernel,
-        out_shape=jax.ShapeDtypeStruct((pair, group, wide), jnp.bfloat16),
-        in_specs=[vmem, pl.BlockSpec(memory_space=pl.ANY)],
-        out_specs=vmem,
-        scratch_shapes=[
-            pltpu.VMEM((ways, pair, group, local), jnp.bfloat16),
-            pltpu.VMEM(w.shape, jnp.bfloat16),
-            pltpu.VMEM((pair, group, wide), jnp.float32),
-            pltpu.VMEM((group, wide), jnp.bfloat16),
-            dma, dma((40,)), dma((ways, 2)), dma((2,)),
-        ],
-        compiler_params=pltpu.CompilerParams(
-            collective_id=collective_id, has_side_effects=True, vmem_limit_bytes=32 << 20
-        ),
-        cost_estimate=pl.CostEstimate(
-            flops=2 * pair * group * ways * local * wide, bytes_accessed=10**7, transcendentals=0
-        ),
-    )(x, w)
-
-
 def body(x, w_in, w_rate, scale, gain, a0, b0, w_out):
     ways = lax.axis_size("head")
     local = x.shape[2]
     w_in = w_in.reshape(ways, local, w_in.shape[2])
     rate = w_rate.astype(jnp.float32).reshape(ways, 1, local)
-    head_out, mixing = front(scale, gain, x, w_in, rate, a0[0], b0[0], w_out[0], 1)
-    return mix(head_out, mixing, 2)
+    return layer(scale, gain, x, w_in, rate, a0[0], b0[0], w_out[0], 1)
 
 
 def solution(mesh):

time: 157 us -> 143 us (0.911)
  Pallas kernels: 149 us -> 137 us
  local copies, waits for them, and re-layouts: 6.18 us -> 4.59 us
    pallas_call x2 -> x1, Pallas kernels: 149 us -> 137 us  [layer(): pl.pallas_call(layer_kernel, out_shape=jax.ShapeDtypeStruct(x.shape, bf16...]
    unnamed x11 -> x9, local copies, waits for them, and re-layouts: 6.18 us -> 4.59 us
where the time goes in v5:
time: 143 us
  Pallas kernels  137 us (96%)
  local copies, waits for them, and re-layouts  4.59 us (3%)
    pallas_call x1, Pallas kernels, layer(): pl.pallas_call(layer_kernel, out_shape=jax.ShapeDtypeStruct(x.shape, bf16...  137 us
    unnamed x9, local copies, waits for them, and re-layouts  4.59 us

profile of v5, /device:TPU:16, one launch (start us, length us, event | category | flops | bytes accessed | tf_op | source)
XLA Modules:
  0.0 142.6 jit_solution(16061597533676279782)
XLA Ops:
  0.7 0.7 convert.1.rate_ref
  1.4 0.0 copy-start
  1.4 1.0 copy-done
  2.4 0.0 copy-start.1
  2.4 1.0 copy-done.1
  3.5 0.0 copy-start.2
  3.5 1.0 copy-done.2
  4.5 0.0 copy-start.3
  4.5 0.7 copy-done.3
  5.2 136.6 %shard_map.82 = bf16[2,512,256]{2,1,0:T(8,128)(2,1)S(1)} custom-call(f32[1]{0:T(128)S(6)} %copy.10.scale_ref, f32[1,256]{1,0:T(1,128)S(1)} %copy-done.3, bf16[2,512,256]{2,1,0:T(8,128)(2,1)S(1)} %copy-done, bf16[16,256,768]{2,1,0:T(8,128)(2,1)} %bitcast.9, f32[16,1,256]{2,1,0:T(1,128)S(1)} %convert.1.rate_ref, f32[256,512]{1,0:T(8,128)S(1)} %bitcast.6, ...), custom_call_target="tpu_custom_call" | custom-call | flops 20000000000 | bytes 10000000 | tf_op jit(solution)/shard_map/pallas_call | solution.py:336
  141.8 0.8 copy.11
Async XLA Ops:
  1.4 1.0 copy-start
  2.4 1.0 copy-start.1
  3.5 1.0 copy-start.2
  4.5 0.7 copy-start.3

commit v6 on v5

--- a/solution.py
+++ b/solution.py
@@ -30,8 +30,8 @@
     return 0.5 * jnp.tanh(0.5 * a) + 0.5
 
 
-def unit_scaled(update):
-    return update * lax.rsqrt(jnp.sum(update * update) + 1e-06)
+def unit_scale(update):
+    return lax.rsqrt(jnp.sum(update * update) + 1e-06)
 
 
 def chain_step(state_a, state_b, k, g):
@@ -40,12 +40,16 @@
     gate = sigmoid(hidden)
     act = half(hidden * gate)
     slopes = half(back * gate * (1.0 + hidden * (1.0 - gate)))
-    xa = unit_scaled(mm(k, slopes, TN))
-    xb = unit_scaled(mm(g, act, TN))
-    for _ in range(NS_STEPS):
+    ua, ub = mm(k, slopes, TN), mm(g, act, TN)
+    ha, hb = half(ua), half(ub)
+    ga, gb = mm(ha, ha, NT), mm(hb, hb, NT)
+    sa, sb = unit_scale(ua), unit_scale(ub)
+    xa, xb = ua * sa, ub * sb
+    gram_a, gram_b = half(ga * sa * sa), half(gb * sb * sb)
+    for i in range(NS_STEPS):
         ha, hb = half(xa), half(xb)
-        gram_a = half(mm(ha, ha, NT))
-        gram_b = half(mm(hb, hb, NT))
+        if i:
+            gram_a, gram_b = half(mm(ha, ha, NT)), half(mm(hb, hb, NT))
         xa = 1.5 * xa - 0.5 * mm(gram_a, ha)
         xb = 1.5 * xb - 0.5 * mm(gram_b, hb)
     state_a[...] += UPDATE_RATE * xa
@@ -62,7 +66,7 @@
     state_a, state_b, top, total, acc,
     mix_ref, heads, held_heads, mixed, stage,
     w_sem, send_sem, recv_sem, out_sem, win_sem, mix_send, mix_recv, mix_own,
-    send_heads, recv_heads, swap_sem,
+    send_heads, recv_heads, swap_sem, b_rows, gain_row, fetch_sem,
 ):
     p = lax.axis_index("seq")
     h = lax.axis_index("head")
@@ -77,6 +81,12 @@
 
     load = pltpu.make_async_copy(w_hbm, weights, w_sem)
     load.start()
+    fetches = [
+        pltpu.make_async_copy(src, dst, fetch_sem.at[i])
+        for i, (src, dst) in enumerate(((a0_ref, state_a), (b0_ref, b_rows), (gain_ref, gain_row)))
+    ]
+    for fetch in fetches:
+        fetch.start()
     barrier = pltpu.get_barrier_semaphore()
     pl.semaphore_signal(barrier, inc=1, device_id=(2 * y + 1 - plane, h), device_id_type=MESH)
     for d in range(1, ways):
@@ -119,6 +129,34 @@
             pl.when(goes_back(row))(back_copy(row, which).start)
             pl.when(goes_next())(next_copy(row, which).start)
 
+    def arrive(slot, j):
+        for which in range(3):
+            pltpu.make_async_remote_copy(
+                src_ref=pieces[which][1].at[slot, j], dst_ref=pieces[which][1].at[slot, j],
+                send_sem=out_sem.at[0, 0, which], recv_sem=win_sem.at[slot, j, which],
+                device_id=(place(y + 1), h), device_id_type=MESH,
+            ).wait_recv()
+
+    def relay(slot, j, target):
+        for which in range(3):
+            outgoing(relayed, j, which, pieces[which][1].at[slot, j], target, 1).start()
+
+    def relays(j):
+        @pl.when((y == 0) & (j == 0))
+        def _():
+            arrive(2, 0)
+            relay(2, 0, y - 1)
+
+        @pl.when((y == 2) & (j == 1))
+        def _():
+            arrive(0, 1)
+            relay(0, 1, y + 1)
+
+        @pl.when(y == 3)
+        def _():
+            arrive(2, j)
+            relay(2, j, y - 1)
+
     def each(t, chunk, block):
         rate = rate_ref[chunk]
         wide = block.astype(jnp.float32)
@@ -130,7 +168,7 @@
     side[...] = jnp.zeros_like(side)
     gather(
         p, h, plane, early, True, SPLIT_IN, x_ref, held, weights, pacc, load.wait, send_sem, recv_sem,
-        each, lambda: project(0, early),
+        each, lambda: project(0, early), fetch_sem.at[3],
     )
     project(1, late)
 
@@ -150,8 +188,9 @@
     for d in range(1, ways):
         mixing(d).start()
 
-    state_a[...] = a0_ref[...]
-    state_b[...] = b0_ref[...].T
+    for fetch in fetches:
+        fetch.wait()
+    state_b[...] = b_rows[...].T
 
     sharp = scale_ref[0] * LOG2E
     tile = group // 2
@@ -185,18 +224,6 @@
         total[j, rows] = total[j, rows] * shrink + jnp.sum(w, axis=1, keepdims=True)
         acc[j, rows] = acc[j, rows] * shrink + mm(half(w), values)
 
-    def arrive(slot, j):
-        for which in range(3):
-            pltpu.make_async_remote_copy(
-                src_ref=pieces[which][1].at[slot, j], dst_ref=pieces[which][1].at[slot, j],
-                send_sem=out_sem.at[0, 0, which], recv_sem=win_sem.at[slot, j, which],
-                device_id=(place(y + 1), h), device_id_type=MESH,
-            ).wait_recv()
-
-    def relay(slot, j, target):
-        for which in range(3):
-            outgoing(relayed, j, which, pieces[which][1].at[slot, j], target, 1).start()
-
     def learn(k, v, t):
         steps = t.T[:, :1]
         chain_step(state_a, state_b, k, half(v.astype(jnp.float32) * steps))
@@ -216,6 +243,7 @@
         lax.fori_loop(0, 2 * pair, turn, 0)
 
     lax.fori_loop(0, 2 * pair, first, 0)
+    relays(early)
 
     def own(r, carry):
         fold(1, r, k_ref[0], v_ref[0], 0)
@@ -223,33 +251,31 @@
 
     lax.fori_loop(0, 2, own, 0)
 
-    @pl.when(y == 0)
+    @pl.when(y < 3)
     def _():
-        arrive(2, 0)
-        relay(2, 0, y - 1)
+        relays(late)
 
     @pl.when(y == 2)
     def _():
-        arrive(0, 1)
-        relay(0, 1, y + 1)
         arrive(0, 0)
-
-    @pl.when(y == 3)
-    def _():
-        arrive(2, early)
-        relay(2, early, y - 1)
 
     @pl.when((y == 1) | (y == 3))
     def _():
         arrive(0, early)
 
-    pl.when(y >= 1)(lambda: near(early))
+    pl.when((y == 1) | (y == 2))(lambda: near(early))
 
     @pl.when(y == 3)
     def _():
-        arrive(2, late)
-        relay(2, late, y - 1)
-        learn_pair(2)
+        relays(late)
+
+        def both(j, carry):
+            learn(kwin[2, j], vwin[2, j], twin_ref[2, j])
+            for r in range(2):
+                fold(j, r, kwin[0, early], vwin[0, early], 0)
+            return carry
+
+        lax.fori_loop(0, pair, both, 0)
 
     @pl.when((y == 1) | (y == 3))
     def _():
@@ -279,7 +305,7 @@
         act = half(hidden * sigmoid(hidden))
         fast = mm(act, half(state_b[...]), NT)
         fast = fast * lax.rsqrt(jnp.mean(fast * fast, axis=1, keepdims=True) + 1e-05)
-        heads[j] = half(acc[j] / total[j] + fast * gain_ref[...])
+        heads[j] = half(acc[j] / total[j] + fast * gain_row[...])
         return carry
 
     for j in range(pair):
@@ -328,7 +354,7 @@
     ways = lax.axis_size("head")
     ring = lax.axis_size("seq") // 2
     vmem = pl.BlockSpec(memory_space=pltpu.VMEM)
-    hbm = pl.BlockSpec(memory_space=pl.ANY)
+    hbm = pl.BlockSpec(memory_space=pltpu.HBM)
     dma = pltpu.SemaphoreType.DMA
     bf16, f32 = jnp.bfloat16, jnp.float32
     block = pltpu.VMEM((pair, group, width), bf16)
@@ -336,7 +362,7 @@
     return pl.pallas_call(
         layer_kernel,
         out_shape=jax.ShapeDtypeStruct(x.shape, bf16),
-        in_specs=[pl.BlockSpec(memory_space=pltpu.SMEM), vmem, vmem, hbm, vmem, vmem, vmem, hbm],
+        in_specs=[pl.BlockSpec(memory_space=pltpu.SMEM), hbm, hbm, hbm, vmem, hbm, hbm, hbm],
         out_specs=vmem,
         scratch_shapes=[
             pltpu.VMEM((ways, pair, group, width), bf16),
@@ -361,9 +387,10 @@
             dma((3, pair, 3)), dma((ring - 1, pair, 3)),
             dma((ways,)), dma((ways,)), dma,
             dma((40 * SPLIT_OUT,)), dma((ways, 2, SPLIT_OUT)), dma((2,)),
+            pltpu.VMEM(b0.shape, f32), pltpu.VMEM(gain.shape, f32), dma((4,)),
         ],
         compiler_params=pltpu.CompilerParams(
-            collective_id=collective_id, has_side_effects=True, vmem_limit_bytes=50 << 20
+            collective_id=collective_id, has_side_effects=True, vmem_limit_bytes=62 << 20
         ),
         cost_estimate=pl.CostEstimate(
             flops=2 * 10**10, bytes_accessed=10**7, transcendentals=10**6
@@ -372,7 +399,7 @@
 
 
 def gather(
-    p, me, plane, first, inward, split, x_ref, held, weights, acc, ready, send_sem, recv_sem, each, middle
+    p, me, plane, first, inward, split, x_ref, held, weights, acc, ready, send_sem, recv_sem, each, middle, swap_sem=None
 ):
     partner = 2 * (p // 2) + 1 - plane
     x, z, core = me // 4, (me // 2) % 2, me % 2
@@ -415,7 +442,11 @@
         for other in (minus, plus, across, twin):
             send(me, 1, (p, other), x_ref.at[1 - first])
         held[me, 1] = x_ref[1 - first]
-    held[me, 0] = x_ref[first]
+    if inward:
+        own = pltpu.make_async_copy(x_ref.at[first], held.at[me, 0], swap_sem)
+        own.start()
+    else:
+        held[me, 0] = x_ref[first]
 
     acc[...] = jnp.zeros_like(acc)
     ready()
@@ -445,6 +476,7 @@
     take(0, 1, 0, (plus, minus))
     take(1, 0, 0, ())
     if inward:
+        own.wait()
         for u in range(split):
             arrived(me, 1, (u,))
             for other in (minus, plus, across, twin):

time: 143 us -> 142 us (level)
  local copies, waits for them, and re-layouts: 4.59 us -> 1.87 us
    unnamed x9 -> x1, local copies, waits for them, and re-layouts: 4.59 us -> 1.87 us
where the time goes in v6:
time: 142 us; the launch traced here: 141 us
  Pallas kernels  137 us (96%)
  local copies, waits for them, and re-layouts  1.87 us (1%)
    pallas_call x1, Pallas kernels, layer(): pl.pallas_call(layer_kernel, out_shape=jax.ShapeDtypeStruct(x.shape, bf16...  137 us

profile of v6, /device:TPU:16, one launch (start us, length us, event | category | flops | bytes accessed | tf_op | source)
XLA Modules:
  0.0 141.3 jit_solution(18412899528802579491)
XLA Ops:
  0.7 1.3 convert.1.rate_ref
  2.0 137.5 %shard_map.82 = bf16[2,512,256]{2,1,0:T(8,128)(2,1)} custom-call(f32[1]{0:T(128)S(6)} %copy.10.scale_ref, f32[1,256]{1,0:T(1,128)} %gain_ref.1, bf16[2,512,256]{2,1,0:T(8,128)(2,1)} %x_ref.1, bf16[16,256,768]{2,1,0:T(8,128)(2,1)} %bitcast.7, f32[16,1,256]{2,1,0:T(1,128)} %convert.1.rate_ref, f32[256,512]{1,0:T(8,128)} %bitcast.9, f32[512,256]{1,0:T(8,128)} %bitcast.10, ...), custom_call_target="tpu_custom_call" | custom-call | flops 20000000000 | bytes 10000000 | tf_op jit(solution)/shard_map/pallas_call | solution.py:362
  139.5 1.9 %copy.11 = bf16[2,512,256]{2,1,0:T(8,128)(2,1)} copy(bf16[2,512,256]{2,1,0:T(8,128)(2,1)} %shard_map.82) | data formatting | bytes 1048576

commit v7 on v6

--- a/solution.py
+++ b/solution.py
@@ -127,6 +127,7 @@
         t_ref[row] = jnp.broadcast_to(step, (group, 128)).T[:8]
         for which in range(3):
             pl.when(goes_back(row))(back_copy(row, which).start)
+        for which in range(3):
             pl.when(goes_next())(next_copy(row, which).start)
 
     def arrive(slot, j):

time: 142 us -> 142 us (level)
  no operation moved by 1% of the time
where the time goes in v7:
time: 142 us; the launch traced here: 141 us
  Pallas kernels  137 us (96%)
  local copies, waits for them, and re-layouts  1.87 us (1%)
    pallas_call x1, Pallas kernels, layer(): pl.pallas_call(layer_kernel, out_shape=jax.ShapeDtypeStruct(x.shape, bf16...  137 us

profile of v7, /device:TPU:16, one launch (start us, length us, event | category | flops | bytes accessed | tf_op | source)
XLA Modules:
  0.0 141.3 jit_solution(8852147198165732793)
XLA Ops:
  0.7 1.3 convert.1.rate_ref
  2.0 137.5 %shard_map.82 = bf16[2,512,256]{2,1,0:T(8,128)(2,1)} custom-call(f32[1]{0:T(128)S(6)} %copy.10.scale_ref, f32[1,256]{1,0:T(1,128)} %gain_ref.1, bf16[2,512,256]{2,1,0:T(8,128)(2,1)} %x_ref.1, bf16[16,256,768]{2,1,0:T(8,128)(2,1)} %bitcast.7, f32[16,1,256]{2,1,0:T(1,128)} %convert.1.rate_ref, f32[256,512]{1,0:T(8,128)} %bitcast.9, f32[512,256]{1,0:T(8,128)} %bitcast.10, ...), custom_call_target="tpu_custom_call" | custom-call | flops 20000000000 | bytes 10000000 | tf_op jit(solution)/shard_map/pallas_call | solution.py:363
  139.5 1.9 %copy.11 = bf16[2,512,256]{2,1,0:T(8,128)(2,1)} copy(bf16[2,512,256]{2,1,0:T(8,128)(2,1)} %shard_map.82) | data formatting | bytes 1048576
